TPU v7x, 128 devices: a whole 4x4x4 slice. The times are simulated.
128 devices in a mesh: row: 16 (over y_hi, z, core), col: 8 (over y_lo, x).
Axes of the slice: x: 4, y: 4 (y_hi: 2, y_lo: 2; y = y_hi * 2 + y_lo), z: 4, core: 2. Of those that a mesh axis runs over, the one named last changes fastest.
Arguments:
- tokens: bfloat16 [16384, 1024], P('row', 'col'), may hold values from -6 to 6
- cotangent: bfloat16 [16384, 1024], P('row', 'col'), may hold values from -6 to 6
- lengths: int32 [32], replicated, may hold values from 0 to 2048, as said below
- deal_order: int32 [16384], replicated, may hold values from 0 to 16383, as said below
- qkv_weight: float32 [1024, 3072], P('col', 'row'), may hold values from -0.1875 to 0.1875
- up_weight: float32 [1024, 4096], P('col', 'row'), may hold values from -0.1875 to 0.1875
- proj_weight: float32 [1024, 1024], P('row', 'col'), may hold values from -1.5 to 1.5
- down_weight: float32 [4096, 1024], P('row', 'col'), may hold values from -0.09375 to 0.09375
- norm_vectors: float32 [3, 1024], P(None, 'col'), may hold values from -0.5 to 1.4, as said below
- qkv_bias: float32 [3072], P('row'), may hold values from -2 to 2
- mlp_bias: float32 [4096], P('row'), may hold values from -2 to 2
- qkv_momentum: float32 [1024, 3072], P('col', 'row'), may hold values from -1536 to 1536
- up_momentum: float32 [1024, 4096], P('col', 'row'), may hold values from -256 to 256
- proj_momentum: float32 [1024, 1024], P('row', 'col'), may hold values from -40 to 40
- down_momentum: float32 [4096, 1024], P('row', 'col'), may hold values from -320 to 320
- norm_moment: float32 [3, 1024], P(None, 'col'), may hold values from -224 to 224
- norm_square: float32 [3, 1024], P(None, 'col'), may hold values from 819.2 to 32768
- qkv_bias_moment: float32 [3072], P('row'), may hold values from -160 to 160
- qkv_bias_square: float32 [3072], P('row'), may hold values from 3276.8 to 13107.2
- mlp_bias_moment: float32 [4096], P('row'), may hold values from -32 to 32
- mlp_bias_square: float32 [4096], P('row'), may hold values from 98.304 to 409.6
Outputs:
- output: float32 [16384, 1024], P('row', 'col')
- input_grad: float32 [16384, 1024], P('row', 'col')
- qkv_grad: float32 [1024, 3072], P('col', 'row')
- up_grad: float32 [1024, 4096], P('col', 'row')
- proj_grad: float32 [1024, 1024], P('row', 'col')
- down_grad: float32 [4096, 1024], P('row', 'col')
- new_qkv_momentum: float32 [1024, 3072], P('col', 'row')
- new_up_momentum: float32 [1024, 4096], P('col', 'row')
- new_proj_momentum: float32 [1024, 1024], P('row', 'col')
- new_down_momentum: float32 [4096, 1024], P('row', 'col')
- new_qkv_weight: float32 [1024, 3072], P('col', 'row')
- new_up_weight: float32 [1024, 4096], P('col', 'row')
- new_proj_weight: float32 [1024, 1024], P('row', 'col')
- new_down_weight: float32 [4096, 1024], P('row', 'col')
- new_norm_moment: float32 [3, 1024], P(None, 'col')
- new_norm_square: float32 [3, 1024], P(None, 'col')
- new_norm_vectors: float32 [3, 1024], P(None, 'col')
- new_qkv_bias_moment: float32 [3072], P('row')
- new_qkv_bias_square: float32 [3072], P('row')
- new_qkv_bias: float32 [3072], P('row')
- new_mlp_bias_moment: float32 [4096], P('row')
- new_mlp_bias_square: float32 [4096], P('row')
- new_mlp_bias: float32 [4096], P('row')
Inputs may be any that keep to these rules, and one draw needn't show every extreme that they name: `lengths`: lengths of the sequences in the initial order of tokens; they sum to 16384; zero marks an unused slot; one length is 2048. `deal_order`: A permutation of the tokens. Each aligned block of 2048 dealt positions holds whole sequences, each contiguous and in its own order, at most 4 of them. `norm_vectors`: row 0 between 0.6 and 1.4, rows 1 and 2 between -0.5 and 0.5.
All inputs are finite; a program needn't handle non-finite values.
Results may differ from a plain program's by a relative error of at most 0.012.
Values may be sent and summed in bfloat16 or wider, within the bound.
A program may use at most 192 MiB of HBM per device.

v0:
```python
import math

import jax
import jax.numpy as jnp
from jax import lax
from jax.sharding import PartitionSpec as P

D = 1024
HEAD = 64
ROT = 16
FF = 4096
STEP = 10


highest = lax.Precision.HIGHEST
poly_linear = 3.4445
poly_square = -4.775
poly_cubic = 2.0315
momentum = 0.95
rate_matrix = 0.15
decay_matrix = 0.1
beta_first = 0.9
beta_second = 0.95
rate_vector = 0.2
adam_floor = 1e-08
norm_floor = 1e-05
ortho_floor = 1e-07
masked_score = -1e30


def for_sending(x):

    def short(part):
        return part.astype(jnp.bfloat16) if part.dtype == jnp.float32 else part

    return jax.tree.map(short, x)


def token_places(lengths, anchor):
    seq_ends = jnp.cumsum(lengths)
    before = seq_ends[None, :] <= anchor[:, None]
    seq_ids = jnp.sum(before.astype(jnp.int32), axis=1)
    starts = jnp.sum(jnp.where(before, lengths[None, :], 0), axis=1)
    return (seq_ids, anchor - starts)


def rotary_tables(places):
    half_rot = ROT // 2
    inverse = 1.0 / 10000.0 ** (jnp.arange(half_rot, dtype=jnp.float32) * (2.0 / ROT))
    angles = places.astype(jnp.float32)[:, None] * inverse[None, :]
    return (jnp.cos(angles), jnp.sin(angles))


def rotate(values, cosine, sine):
    half_rot = ROT // 2
    lower_half = values[..., :half_rot]
    upper_half = values[..., half_rot:ROT]
    return jnp.concatenate(
        [
            lower_half * cosine - upper_half * sine,
            upper_half * cosine + lower_half * sine,
            values[..., ROT:],
        ],
        axis=-1,
    )


def gelu_tanh(values):
    return jax.nn.gelu(values, approximate=True)


def block_mask(seq_ids, places, row_start, block_rows):
    query_ids = lax.dynamic_slice_in_dim(seq_ids, row_start, block_rows)
    query_places = lax.dynamic_slice_in_dim(places, row_start, block_rows)
    return (query_ids[:, None] == seq_ids[None, :]) & (places[None, :] <= query_places[:, None])


def attend_forward(queries, keys_all, values_all, seq_ids, places, block_rows):
    score_scale = HEAD ** (-0.5)
    heads_here, group_rows, head_dim = queries.shape
    block_count = group_rows // block_rows

    def one_block(block_index):
        row_start = block_index * block_rows
        query_block = lax.dynamic_slice_in_dim(queries, row_start, block_rows, 1)
        allowed = block_mask(seq_ids, places, row_start, block_rows)
        scores = (
            jnp.einsum("hqd,hkd->hqk", query_block, keys_all, preferred_element_type=jnp.float32)
            * score_scale
        )
        scores = jnp.where(allowed[None], scores, masked_score)
        log_total = jax.nn.logsumexp(scores, axis=-1, keepdims=True)
        weights = jnp.exp(scores - log_total).astype(jnp.bfloat16)
        attended = jnp.einsum(
            "hqk,hkd->hqd", weights, values_all, preferred_element_type=jnp.float32
        )
        return (attended.astype(jnp.bfloat16), log_total[..., 0])

    attended, totals = lax.map(one_block, jnp.arange(block_count, dtype=jnp.int32))
    attended = attended.transpose(1, 0, 2, 3).reshape(heads_here, group_rows, head_dim)
    totals = totals.transpose(1, 0, 2).reshape(heads_here, group_rows)
    return (attended, totals)


def attend_backward(
    queries, keys_all, values_all, attended_grad, totals, seq_ids, places, block_rows
):
    score_scale = HEAD ** (-0.5)
    heads_here, group_rows, head_dim = queries.shape
    block_count = group_rows // block_rows

    def one_block(running, block_index):
        key_grad, value_grad = running
        row_start = block_index * block_rows
        query_block = lax.dynamic_slice_in_dim(queries, row_start, block_rows, 1)
        grad_block = lax.dynamic_slice_in_dim(attended_grad, row_start, block_rows, 1)
        total_block = lax.dynamic_slice_in_dim(totals, row_start, block_rows, 1)
        allowed = block_mask(seq_ids, places, row_start, block_rows)
        scores = (
            jnp.einsum("hqd,hkd->hqk", query_block, keys_all, preferred_element_type=jnp.float32)
            * score_scale
        )
        scores = jnp.where(allowed[None], scores, masked_score)
        probabilities = jnp.exp(scores - total_block[..., None])
        prob_grad = jnp.einsum(
            "hqd,hkd->hqk", grad_block, values_all, preferred_element_type=jnp.float32
        )
        row_delta = jnp.sum(probabilities * prob_grad, axis=-1, keepdims=True)
        score_grad = (probabilities * (prob_grad - row_delta)).astype(jnp.bfloat16)
        query_grad = (
            jnp.einsum("hqk,hkd->hqd", score_grad, keys_all, preferred_element_type=jnp.float32)
            * score_scale
        )
        key_grad = (
            key_grad
            + jnp.einsum(
                "hqk,hqd->hkd", score_grad, query_block, preferred_element_type=jnp.float32
            )
            * score_scale
        )
        value_grad = value_grad + jnp.einsum(
            "hqk,hqd->hkd",
            probabilities.astype(jnp.bfloat16),
            grad_block,
            preferred_element_type=jnp.float32,
        )
        return ((key_grad, value_grad), query_grad)

    zero_grad = jnp.zeros((heads_here, group_rows, head_dim), jnp.float32)
    (key_grad, value_grad), query_grad = lax.scan(
        one_block, (zero_grad, zero_grad), jnp.arange(block_count, dtype=jnp.int32)
    )
    query_grad = query_grad.transpose(1, 0, 2, 3).reshape(heads_here, group_rows, head_dim)
    return (query_grad, key_grad, value_grad)


def adam_step(value, gradient, first_state, second_state):
    first_new = beta_first * first_state + (1.0 - beta_first) * gradient
    second_new = beta_second * second_state + (1.0 - beta_second) * gradient * gradient
    corrected = first_new / (1.0 - beta_first**STEP)
    root_term = jnp.sqrt(second_new / (1.0 - beta_second**STEP)) + adam_floor
    return (first_new, second_new, value - rate_vector * corrected / root_term)


def per_device(
    tokens,
    cotangent,
    lengths,
    deal_order,
    qkv_weight,
    up_weight,
    proj_weight,
    down_weight,
    norm_vectors,
    qkv_bias,
    mlp_bias,
    qkv_momentum,
    up_momentum,
    proj_momentum,
    down_momentum,
    norm_moment,
    norm_square,
    qkv_bias_moment,
    qkv_bias_square,
    mlp_bias_moment,
    mlp_bias_square,
):
    columns = lax.axis_size("col")
    total_tokens = deal_order.shape[0]
    group_rows = total_tokens // columns
    qkv_width = qkv_weight.shape[1]
    up_width = up_weight.shape[1]
    heads_here = qkv_width // (3 * HEAD)
    proj_width = heads_here * HEAD
    block_rows = min(512, group_rows)
    inputs = tokens.astype(jnp.float32)
    sum_first, sum_second = lax.psum(
        (jnp.sum(inputs, axis=1), jnp.sum(inputs * inputs, axis=1)), "col"
    )
    mean_row = sum_first / D
    inverse_std = lax.rsqrt(sum_second / D - mean_row * mean_row + norm_floor)
    normalized = (inputs - mean_row[:, None]) * inverse_std[:, None]
    normed = (normalized * norm_vectors[0] + norm_vectors[1]).astype(jnp.bfloat16)
    normed_all = lax.all_gather(normed, "row", axis=0, tiled=True)
    dealt_normed = jnp.take(normed_all, deal_order, axis=0)
    inverse_order = (
        jnp.zeros_like(deal_order).at[deal_order].set(jnp.arange(total_tokens, dtype=jnp.int32))
    )
    in_weight = jnp.concatenate([qkv_weight, up_weight], axis=1).astype(jnp.bfloat16)
    out_weight = jnp.concatenate([proj_weight, down_weight], axis=0).astype(jnp.bfloat16)
    row_piece = dealt_normed
    preact = lax.psum_scatter(
        jnp.dot(row_piece, in_weight, preferred_element_type=jnp.float32),
        "col",
        scatter_dimension=0,
        tiled=True,
    )
    pre_qkv = preact[:, :qkv_width] + qkv_bias
    pre_up = preact[:, qkv_width:] + mlp_bias
    anchor = lax.dynamic_slice_in_dim(deal_order, lax.axis_index("col") * group_rows, group_rows)
    seq_ids, places = token_places(lengths, anchor)
    cosine, sine = rotary_tables(places)
    split_heads = pre_qkv.reshape(group_rows, heads_here, 3, HEAD).transpose(2, 1, 0, 3)
    queries = rotate(split_heads[0], cosine, sine).astype(jnp.bfloat16)
    keys_all = rotate(split_heads[1], cosine, sine).astype(jnp.bfloat16)
    values_all = split_heads[2].astype(jnp.bfloat16)
    attended, totals = attend_forward(queries, keys_all, values_all, seq_ids, places, block_rows)
    activated, gelu_back = jax.vjp(gelu_tanh, pre_up)
    branch = jnp.concatenate(
        [
            attended.transpose(1, 0, 2).reshape(group_rows, proj_width),
            activated.astype(jnp.bfloat16),
        ],
        axis=1,
    )

    def gather_branch():
        return lax.all_gather(branch, "col", axis=0, tiled=True)

    branch_all = gather_branch()
    branch_orig = jnp.take(branch_all, inverse_order, axis=0)
    row_piece = branch_orig
    branch_sum = lax.psum_scatter(
        jnp.dot(row_piece, out_weight, preferred_element_type=jnp.float32),
        "row",
        scatter_dimension=0,
        tiled=True,
    )
    output = inputs + branch_sum + norm_vectors[2]
    cotangent_all = lax.all_gather(cotangent, "row", axis=0, tiled=True)
    cotangent_dealt = jnp.take(cotangent_all, deal_order, axis=0)
    row_piece = cotangent_dealt
    branch_grad = lax.psum_scatter(
        jnp.dot(row_piece, out_weight.T, preferred_element_type=jnp.float32),
        "col",
        scatter_dimension=0,
        tiled=True,
    )
    branch_back = gather_branch()
    out_weight_grad = lax.dot_general(
        branch_back, cotangent_dealt, (((0,), (0,)), ((), ())), preferred_element_type=jnp.float32
    )
    out_bias_grad = jnp.sum(cotangent_all, axis=0, dtype=jnp.float32)
    attended_grad = (
        branch_grad[:, :proj_width]
        .reshape(group_rows, heads_here, HEAD)
        .transpose(1, 0, 2)
        .astype(jnp.bfloat16)
    )
    up_pre_grad = gelu_back(branch_grad[:, proj_width:])[0]
    query_grad, key_grad, value_grad = attend_backward(
        queries, keys_all, values_all, attended_grad, totals, seq_ids, places, block_rows
    )
    qkv_pre_grad = jnp.stack(
        [rotate(query_grad, cosine, -sine), rotate(key_grad, cosine, -sine), value_grad], axis=0
    )
    qkv_pre_grad = qkv_pre_grad.transpose(2, 1, 0, 3).reshape(group_rows, qkv_width)
    preact_grad = jnp.concatenate([qkv_pre_grad, up_pre_grad], axis=1).astype(jnp.bfloat16)
    preact_grad_all = lax.all_gather(preact_grad, "col", axis=0, tiled=True)
    in_weight_grad = lax.dot_general(
        dealt_normed, preact_grad_all, (((0,), (0,)), ((), ())), preferred_element_type=jnp.float32
    )
    in_bias_grad = jnp.sum(preact_grad_all, axis=0, dtype=jnp.float32)
    preact_grad_orig = jnp.take(preact_grad_all, inverse_order, axis=0)
    row_piece = preact_grad_orig
    normed_grad = lax.psum_scatter(
        jnp.dot(row_piece, in_weight.T, preferred_element_type=jnp.float32),
        "row",
        scatter_dimension=0,
        tiled=True,
    )
    scaled_grad = normed_grad * norm_vectors[0]
    grad_first, grad_second = lax.psum(
        (jnp.sum(scaled_grad, axis=1), jnp.sum(scaled_grad * normalized, axis=1)), "col"
    )
    input_grad = cotangent.astype(jnp.float32) + inverse_std[:, None] * (
        scaled_grad - (grad_first / D)[:, None] - normalized * (grad_second / D)[:, None]
    )
    gain_grad, shift_grad = lax.psum(
        (jnp.sum(normed_grad * normalized, axis=0), jnp.sum(normed_grad, axis=0)), "row"
    )
    gradients = (
        in_weight_grad[:, :qkv_width],
        in_weight_grad[:, qkv_width:],
        out_weight_grad[:proj_width],
        out_weight_grad[proj_width:],
    )
    old_states = (qkv_momentum, up_momentum, proj_momentum, down_momentum)
    weights = (qkv_weight, up_weight, proj_weight, down_weight)
    flip_flags = (False, False, True, True)
    widths = (3 * D, FF, D, FF)
    states = [momentum * old_state + gradient for old_state, gradient in zip(old_states, gradients)]
    oriented = []
    owner_widths = []
    for gradient, state, flipped in zip(gradients, states, flip_flags):
        direction = gradient + momentum * state
        direction = direction.T if flipped else direction
        owner_widths.append(direction.shape[1])
        oriented.append(jnp.pad(direction, ((0, 0), (0, up_width - direction.shape[1]))))
    oriented = oriented + [jnp.zeros_like(oriented[0])] * (columns - 4)
    incoming = lax.all_to_all(
        jnp.stack(oriented, axis=0), "col", split_axis=0, concat_axis=0, tiled=True
    )
    matrix = incoming.reshape(-1, up_width)
    for sweep_index in range(5):
        gram_matrix = lax.psum(jnp.dot(matrix, matrix.T, precision=highest), "row")
        if sweep_index == 0:
            shrink = 1.0 / (jnp.sqrt(jnp.trace(gram_matrix)) + ortho_floor)
            matrix = matrix * shrink
            gram_matrix = gram_matrix * (shrink * shrink)
        applied = jnp.dot(gram_matrix, matrix, precision=highest)
        matrix = (
            poly_linear * matrix
            + poly_square * applied
            + poly_cubic * jnp.dot(gram_matrix, applied, precision=highest)
        )
    returned = lax.all_to_all(
        for_sending(matrix.reshape(columns, -1, up_width)),
        "col",
        split_axis=0,
        concat_axis=0,
        tiled=True,
    )
    new_weights = []
    for matrix_index in range(4):
        update = returned[matrix_index][:, : owner_widths[matrix_index]]
        update = update.T if flip_flags[matrix_index] else update
        new_weights.append(
            weights[matrix_index] * (1.0 - rate_matrix * decay_matrix)
            - rate_matrix * 0.2 * math.sqrt(widths[matrix_index]) * update
        )
    norm_grads = jnp.stack([gain_grad, shift_grad, out_bias_grad], axis=0)
    norm_first, norm_second, norm_new = adam_step(
        norm_vectors, norm_grads, norm_moment, norm_square
    )
    qkv_first, qkv_second, qkv_bias_new = adam_step(
        qkv_bias, in_bias_grad[:qkv_width], qkv_bias_moment, qkv_bias_square
    )
    mlp_first, mlp_second, mlp_bias_new = adam_step(
        mlp_bias, in_bias_grad[qkv_width:], mlp_bias_moment, mlp_bias_square
    )
    return (
        output,
        input_grad,
        gradients[0],
        gradients[1],
        gradients[2],
        gradients[3],
        states[0],
        states[1],
        states[2],
        states[3],
        new_weights[0],
        new_weights[1],
        new_weights[2],
        new_weights[3],
        norm_first,
        norm_second,
        norm_new,
        qkv_first,
        qkv_second,
        qkv_bias_new,
        mlp_first,
        mlp_second,
        mlp_bias_new,
    )


def solution(mesh):
    return jax.shard_map(
        per_device,
        mesh=mesh,
        in_specs=(
            P("row", "col"),
            P("row", "col"),
            P(),
            P(),
            P("col", "row"),
            P("col", "row"),
            P("row", "col"),
            P("row", "col"),
            P(None, "col"),
            P("row"),
            P("row"),
            P("col", "row"),
            P("col", "row"),
            P("row", "col"),
            P("row", "col"),
            P(None, "col"),
            P(None, "col"),
            P("row"),
            P("row"),
            P("row"),
            P("row"),
        ),
        out_specs=(
            P("row", "col"),
            P("row", "col"),
            P("col", "row"),
            P("col", "row"),
            P("row", "col"),
            P("row", "col"),
            P("col", "row"),
            P("col", "row"),
            P("row", "col"),
            P("row", "col"),
            P("col", "row"),
            P("col", "row"),
            P("row", "col"),
            P("row", "col"),
            P(None, "col"),
            P(None, "col"),
            P(None, "col"),
            P("row"),
            P("row"),
            P("row"),
            P("row"),
            P("row"),
            P("row"),
        ),
        check_vma=False,
    )
```

profile of v0, /device:TPU:0, one launch (start us, length us, event | category | flops | bytes accessed | tf_op | source)
XLA Modules:
  0.0 2000.4 jit_solution(2655185559985852625)
XLA Ops:
  9.8 20.1 %all-reduce.4 = (f32[1024]{0:T(1024)S(1)}, f32[1024]{0:T(1024)S(1)}) all-reduce(f32[1024]{0:T(1024)S(1)} %get-tuple-element.361, f32[1024]{0:T(1024)S(1)} %get-tuple-element.360), channel_id=1, replica_groups=mesh['row'=16,'col'=8] {'col'}, use_global_device_ids=true, to_apply=%region_4.5 | all-reduce | flops 2048 | bytes 16384 | tf_op jit(solution)/shard_map/psum | solution.py:197
  37.6 50.1 %all-gather.5.cloned.1.call-done = bf16[16384,128]{1,0:T(8,128)(2,1)} async-done(((bf16[1024,128]{1,0:T(8,128)(2,1)}), bf16[16384,128]{1,0:T(8,128)(2,1)}) %all-gather.5.cloned.1.call-update) | async-done | bytes 4194320 | tf_op jit(solution)/shard_map/all_gather | solution.py:204
  87.7 57.6 %gather_fusion.2 = bf16[16384,128]{1,0:T(8,128)(2,1)} fusion(bf16[16384,128]{1,0:T(8,128)(2,1)} %all-gather.5.cloned.1.call-done, s32[16384]{0:T(1024)S(1)} %get-tuple-element.458), kind=kCustom, calls=%fused_computation.clone | custom fusion | bytes 8454144 | tf_op jit(solution)/shard_map/jit(_take)/gather | solution.py:205
  158.8 57.6 %gather_fusion.3 = bf16[16384,128]{1,0:T(8,128)(2,1)} fusion(bf16[16384,128]{1,0:T(8,128)(2,1)} %all-gather.9.cloned.1.call-done, s32[16384]{0:T(1024)S(1)} %get-tuple-element.458), kind=kCustom, calls=%fused_computation.1.clone | custom fusion | bytes 8454144 | tf_op jit(solution)/shard_map/jit(_take)/gather | solution.py:251
  229.2 216.2 %reduce-scatter.5.cloned.1.call-done = f32[2048,448]{0,1:T(8,128)} async-done(((f32[16384,448]{0,1:T(8,128)}), f32[2048,448]{0,1:T(8,128)}) %reduce-scatter.5.cloned.1.call-update) | async-done | bytes 3670032 | tf_op jit(solution)/shard_map/reduce_scatter | solution.py:212
  448.4 27.4 %while.27 = (s32[]{:T(128)}, bf16[4,1,512,64]{2,3,1,0:T(8,128)(2,1)S(1)}, f32[4,1,512]{2,1,0:T(1,128)}, s32[4]{0:T(128)S(1)}, s32[2048]{0:T(1024)}, /*index=5*/s...) while((s32[]{:T(128)}, ...), condition=%wide.region_12.14_spmd, body=%wide.region_9.13_spmd.sunk | while | flops 278957568 | bytes 13883603 | solution.py:99
  476.1 181.2 %reduce-scatter.9.cloned.1.call-done = f32[2048,320]{0,1:T(8,128)} async-done(((f32[16384,320]{0,1:T(8,128)}), f32[2048,320]{0,1:T(8,128)}) %reduce-scatter.9.cloned.1.call-update) | async-done | bytes 2621456 | tf_op jit(solution)/shard_map/reduce_scatter | solution.py:253
  664.2 54.3 %while.28 = (s32[]{:T(128)}, f32[1,2048,64]{1,2,0:T(8,128)S(1)}, f32[1,2048,64]{1,2,0:T(8,128)S(1)}, f32[4,1,512,64]{2,0,3,1:T(4,128)}, s32[4]{0:T(128)}, /*inde...) while((s32[]{:T(128)}, f32[1,2048,64]{1,2,0:T(8,128)S(1)}, ...), condition=%wide.region_17.19_spmd.clone, body=%wide.region_15.18_spmd.clone.sunk | while | flops 684359168 | bytes 37001500 | solution.py:150
  722.8 50.1 %all-gather.7.cloned.1.call-done = bf16[16384,320]{0,1:T(8,128)(2,1)} async-done(((bf16[2048,320]{0,1:T(8,128)(2,1)}), bf16[16384,320]{0,1:T(8,128)(2,1)}) %all-gather.7.cloned.1.call-update) | async-done | bytes 10485776 | tf_op jit(solution)/shard_map/all_gather | solution.py:238
  781.8 142.3 %all-gather.11.cloned.1.call-done = bf16[16384,448]{0,1:T(8,128)(2,1)} async-done(((bf16[2048,448]{0,1:T(8,128)(2,1)}), bf16[16384,448]{0,1:T(8,128)(2,1)}) %all-gather.11.cloned.1.call-update) | async-done | bytes 14680080 | tf_op jit(solution)/shard_map/all_gather | solution.py:279
  933.9 18.4 all_to_all.10
  957.9 149.6 %all-reduce.11.cloned.1.call-done = f32[1024,1024]{1,0:T(8,128)} async-done(((f32[1024,1024]{1,0:T(8,128)}), f32[1024,1024]{1,0:T(8,128)}) %all-reduce.11.cloned.1.call-update) | async-done | bytes 4194320 | tf_op jit(solution)/shard_map/psum | solution.py:326
  1125.5 151.4 %all-reduce.13.cloned.1.call-done = f32[1024,1024]{1,0:T(8,128)} async-done(((f32[1024,1024]{1,0:T(8,128)}), f32[1024,1024]{1,0:T(8,128)}) %all-reduce.13.cloned.1.call-update) | async-done | bytes 4194320 | tf_op jit(solution)/shard_map/psum | solution.py:326
  1291.2 151.1 %all-reduce.15.cloned.1.call-done = f32[1024,1024]{1,0:T(8,128)} async-done(((f32[1024,1024]{1,0:T(8,128)}), f32[1024,1024]{1,0:T(8,128)}) %all-reduce.15.cloned.1.call-update) | async-done | bytes 4194320 | tf_op jit(solution)/shard_map/psum | solution.py:326
  1456.5 60.8 %scatter_custom_fusion = s32[16384]{0:T(1024)S(1)} fusion(s32[16384]{0:T(1024)} %get-tuple-element.457, s32[16384]{0:T(1024)S(1)} %iota.28, s32[]{:T(128)} %constant.58.clone.1), kind=kCustom, calls=%fused_computation.208 | custom fusion | bytes 66048 | tf_op jit(solution)/shard_map/scatter | solution.py:207
  1517.4 20.2 %copy.128 = bf16[16384,448]{1,0:T(8,128)(2,1)} copy(bf16[16384,448]{0,1:T(8,128)(2,1)} %all-gather.11.cloned.1.call-done) | data formatting | bytes 29360128 | tf_op jit(solution)/shard_map/all_gather | solution.py:279
  1537.6 74.8 %gather_fusion.1 = bf16[16384,448]{1,0:T(8,128)(2,1)} fusion(bf16[16384,448]{1,0:T(8,128)(2,1)} %copy.128, s32[16384]{0:T(1024)S(1)} %fusion.126), kind=kCustom, calls=%fused_computation.3 | custom fusion | bytes 29425664 | tf_op jit(solution)/shard_map/jit(_take)/gather | solution.py:284
  1612.4 13.5 fusion.34
  1640.8 16.3 copy.122
  1657.1 70.1 %gather_fusion = bf16[16384,320]{1,0:T(8,128)(2,1)} fusion(bf16[16384,320]{1,0:T(8,128)(2,1)} %copy.122, s32[16384]{0:T(1024)S(1)} %fusion.126), kind=kCustom, calls=%fused_computation.2 | custom fusion | bytes 21037056 | tf_op jit(solution)/shard_map/jit(_take)/gather | solution.py:241
  1757.0 38.1 %all-reduce.2 = (f32[1,128]{1,0:T(1,128)S(1)}, f32[1,128]{1,0:T(1,128)S(1)}) all-reduce(f32[1,128]{1,0:T(1,128)S(1)} %bitcast.219, f32[1,128]{1,0:T(1,128)S(1)} %bitcast.218), channel_id=1, replica_groups=mesh['row'=16,'col'=8] {'row'}, use_global_device_ids=true, to_apply=%region_32.34 | all-reduce | flops 256 | bytes 2048 | tf_op jit(solution)/shard_map/psum | solution.py:299
  1795.1 19.1 all-reduce.3
  1814.8 66.2 %all-reduce.19.cloned.1.call-done = f32[1024,1024]{1,0:T(8,128)} async-done(((f32[1024,1024]{1,0:T(8,128)}), f32[1024,1024]{1,0:T(8,128)}) %all-reduce.19.cloned.1.call-update) | async-done | bytes 4194320 | tf_op jit(solution)/shard_map/psum | solution.py:326
  1895.3 93.0 %reduce-scatter.7.cloned.1.call-done = f32[1024,128]{1,0:T(8,128)} async-done(((f32[16384,128]{1,0:T(8,128)}), f32[1024,128]{1,0:T(8,128)}) %reduce-scatter.7.cloned.1.call-update) | async-done | bytes 524304 | tf_op jit(solution)/shard_map/reduce_scatter | solution.py:243
  (327 shorter events, 261.3 us)
Async XLA Ops:
  7.2 80.5 %all-gather.5.cloned.1.call-start = ((), (), s32[]{:S(2)}) async-start(), calls=%async_computation.6 | async-start | bytes 4456448 | tf_op jit(solution)/shard_map/all_gather | solution.py:204
  32.5 126.3 %all-gather.9.cloned.1.call-start = ((), (), s32[]{:S(2)}) async-start(), calls=%async_computation.10 | async-start | bytes 4456448 | tf_op jit(solution)/shard_map/all_gather | solution.py:250
  33.2 412.1 %reduce-scatter.5.cloned.1.call-start = ((), (), s32[]{:S(2)}) async-start(), calls=%async_computation.7 | async-start | bytes 33030144 | tf_op jit(solution)/shard_map/reduce_scatter | solution.py:212
  34.3 111.1 %copy-start.18 = (bf16[128,192]{1,0:T(8,128)(2,1)}, bf16[128,192]{1,0:T(8,128)(2,1)S(1)}, u32[]{:S(2)}) copy-start(bf16[128,192]{1,0:T(8,128)(2,1)S(1)} %copy.116) | copy-start | bytes 147460
  35.3 110.1 %copy-start.16 = (bf16[128,256]{1,0:T(8,128)(2,1)}, bf16[128,256]{1,0:T(8,128)(2,1)S(1)}, u32[]{:S(2)}) copy-start(bf16[128,256]{1,0:T(8,128)(2,1)S(1)} %convert.77) | copy-start | bytes 196612
  157.8 499.4 %reduce-scatter.9.cloned.1.call-start = ((), (), s32[]{:S(2)}) async-start(), calls=%async_computation.11 | async-start | bytes 23592960 | tf_op jit(solution)/shard_map/reduce_scatter | solution.py:253
  226.1 219.3 %copy-start.36 = (f32[192]{0:T(256)S(1)}, f32[192]{0:T(256)}, u32[]{:S(2)}) copy-start(f32[192]{0:T(256)} %param.36) | copy-start | bytes 2308
  226.1 546.8 %all-gather.7.cloned.1.call-start = ((), (), s32[]{:S(2)}) async-start(), calls=%async_computation.8 | async-start | bytes 11796480 | tf_op jit(solution)/shard_map/all_gather | solution.py:238
  227.1 220.7 %copy-start.40 = (f32[8]{0:T(128)}, f32[8]{0:T(128)S(1)}, u32[]{:S(2)}) copy-start(f32[8]{0:T(128)S(1)} %negate_power_fusion) | copy-start | bytes 100
  229.2 218.3 %copy-start.25 = (f32[2048]{0:T(1024)}, f32[2048]{0:T(1024)S(1)}, u32[]{:S(2)}) copy-start(f32[2048]{0:T(1024)S(1)} %get-tuple-element.430) | copy-start | bytes 24580
  448.4 208.9 %copy-start.38 = (f32[256]{0:T(256)S(1)}, f32[256]{0:T(256)}, u32[]{:S(2)}) copy-start(f32[256]{0:T(256)} %param.37) | copy-start | bytes 3076
  475.8 186.5 %copy-start.6 = (bf16[1,2048,64]{2,1,0:T(8,128)(2,1)}, bf16[1,2048,64]{2,1,0:T(8,128)(2,1)S(1)}, u32[]{:S(2)}) copy-start(bf16[1,2048,64]{2,1,0:T(8,128)(2,1)S(1)} %get-tuple-element.744) | copy-start | bytes 786436
  662.4 261.7 %all-gather.11.cloned.1.call-start = ((), (), s32[]{:S(2)}) async-start(), calls=%async_computation.12 | async-start | bytes 16515072 | tf_op jit(solution)/shard_map/all_gather | solution.py:279
  722.6 384.9 %all-reduce.11.cloned.1.call-start = ((), (), s32[]{:S(2)}) async-start(), calls=%async_computation.14 | async-start | bytes 8388608 | tf_op jit(solution)/shard_map/psum | solution.py:326
  781.8 151.2 %copy-start.24 = (f32[128,192]{0,1:T(8,128)S(1)}, f32[128,192]{0,1:T(8,128)}, u32[]{:S(2)}) copy-start(f32[128,192]{0,1:T(8,128)} %param.38) | copy-start | bytes 294916
  957.4 319.5 %all-reduce.13.cloned.1.call-start = ((), (), s32[]{:S(2)}) async-start(), calls=%async_computation.15 | async-start | bytes 8388608 | tf_op jit(solution)/shard_map/psum | solution.py:326
  1125.3 317.1 %all-reduce.15.cloned.1.call-start = ((), (), s32[]{:S(2)}) async-start(), calls=%async_computation.16 | async-start | bytes 8388608 | tf_op jit(solution)/shard_map/psum | solution.py:326
  1291.0 335.5 %all-reduce.17.cloned.1.call-start = ((), (), s32[]{:S(2)}) async-start(), calls=%async_computation.17 | async-start | bytes 8388608 | tf_op jit(solution)/shard_map/psum | solution.py:326
  1456.5 298.8 %reduce-scatter.11.cloned.1.call-start = ((), (), s32[]{:S(2)}) async-start(), calls=%async_computation.13 | async-start | bytes 8912896 | tf_op jit(solution)/shard_map/reduce_scatter | solution.py:286
  1625.9 255.1 %all-reduce.19.cloned.1.call-start = ((), (), s32[]{:S(2)}) async-start(), calls=%async_computation.18 | async-start | bytes 8388608 | tf_op jit(solution)/shard_map/psum | solution.py:326
  1640.6 347.7 %reduce-scatter.7.cloned.1.call-start = ((), (), s32[]{:S(2)}) async-start(), calls=%async_computation.9 | async-start | bytes 8912896 | tf_op jit(solution)/shard_map/reduce_scatter | solution.py:243
  1890.0 102.3 %copy-start.13 = (f32[128,192]{0,1:T(8,128)S(1)}, f32[128,192]{0,1:T(8,128)}, u32[]{:S(2)}) copy-start(f32[128,192]{0,1:T(8,128)} %param.31) | copy-start | bytes 294916
  1890.0 102.9 %copy-start.12 = (f32[256,128]{1,0:T(8,128)S(1)}, f32[256,128]{1,0:T(8,128)}, u32[]{:S(2)}) copy-start(f32[256,128]{1,0:T(8,128)} %param.34) | copy-start | bytes 393220
  1891.0 99.8 %all-to-all-start.1 = ((bf16[8,128,256]{1,2,0:T(8,128)(2,1)}), bf16[8,128,256]{1,2,0:T(8,128)(2,1)S(1)}, u32[]{:S(2)}, u32[]{:S(2)}) async-start(bf16[8,128,256]{1,2,0:T(8,128)(2,1)} %copy.134), calls=%async_computation.5 | async-start | bytes 1048576 | tf_op jit(solution)/shard_map/all_to_all | solution.py:337
  (42 other events, 1284.4 us)
Sparse Core Ops, SparseCore 0:
  32.6 55.0 all-gather.4
  90.2 53.1 all-gather.8
  158.0 287.3 reduce-scatter.4
  447.7 209.5 reduce-scatter.8
  662.5 110.3 all-gather.6
  774.4 149.6 all-gather.10
  957.5 149.9 all-reduce.10
  1125.4 151.4 all-reduce.12
  1291.1 151.2 all-reduce.14
  1456.6 151.2 all-reduce.16
  1626.0 102.9 reduce-scatter.10
  1731.5 149.4 all-reduce.18
  1885.3 103.0 reduce-scatter.6
where the time goes:
time: 2010 us; the launch traced here: 2000 us
  waiting for transfers between devices  1250 us (62%)
  local copies, waits for them, and re-layouts  408 us (20%)
  matrix products  166 us (8%)
  blocking collectives  95.7 us (5%)
  other arithmetic  50.6 us (3%)
    psum x5, waiting for transfers between devices, per_device(): gram_matrix = lax.psum(jnp.dot(matrix, matrix.T, precision=highest), 'row')  518 us
    reduce_scatter x1, waiting for transfers between devices, per_device(): lax.psum_scatter(jnp.dot(row_piece, in_weight, preferred_element_type=jnp...  216 us
    reduce_scatter x1, waiting for transfers between devices, per_device(): lax.psum_scatter(jnp.dot(row_piece, out_weight.T, preferred_element_type=...  181 us
    all_gather x1, waiting for transfers between devices, per_device(): preact_grad_all = lax.all_gather(preact_grad, 'col', axis=0, tiled=True)  142 us
    reduce_scatter x1, waiting for transfers between devices, per_device(): lax.psum_scatter(jnp.dot(row_piece, out_weight, preferred_element_type=jn...  93 us
    gather x1, local copies, waits for them, and re-layouts, per_device(): preact_grad_orig = jnp.take(preact_grad_all, inverse_order, axis=0)  74.8 us
    gather x1, local copies, waits for them, and re-layouts, per_device(): branch_orig = jnp.take(branch_all, inverse_order, axis=0)  70.1 us
    scatter x1, local copies, waits for them, and re-layouts, per_device(): jnp.zeros_like(deal_order).at[deal_order]  60.8 us
  transfers between devices with their start and end apart: 14, of which 10 were waited for; matrix products, arithmetic and copies ran while one was open for 27% of the time, Pallas kernels for 0%

commit v1 on v0

v1 whole, which is shorter than its diff:
```python
import functools
import math

import jax
import jax.numpy as jnp
from jax import lax
from jax.experimental import pallas as pl
from jax.experimental.pallas import tpu as pltpu
from jax.sharding import PartitionSpec as P

D = 1024
HEAD = 64
ROT = 16
FF = 4096
STEP = 10

poly_linear = 3.4445
poly_square = -4.775
poly_cubic = 2.0315
momentum = 0.95
rate_matrix = 0.15
decay_matrix = 0.1
beta_first = 0.9
beta_second = 0.95
rate_vector = 0.2
adam_floor = 1e-08
norm_floor = 1e-05
ortho_floor = 1e-07
masked_score = -1e30
high = lax.Precision.HIGH
f32 = jnp.float32
bf16 = jnp.bfloat16
BLOCK = 256
EXTRA = 16


def dot_nt(a, b, **kw):
    return lax.dot_general(a, b, (((1,), (1,)), ((), ())), preferred_element_type=f32, **kw)


def dot_tn(a, b, **kw):
    return lax.dot_general(a, b, (((0,), (0,)), ((), ())), preferred_element_type=f32, **kw)


def dot_nn(a, b, **kw):
    return lax.dot_general(a, b, (((1,), (0,)), ((), ())), preferred_element_type=f32, **kw)


def allowed_keys(start_ref, first, keys):
    shape = (BLOCK, keys)
    key_at = lax.broadcasted_iota(jnp.int32, shape, 1)
    query_at = first + lax.broadcasted_iota(jnp.int32, shape, 0)
    return (key_at >= start_ref[pl.ds(first, BLOCK), :]) & (key_at <= query_at)


def attend_kernel(q_ref, k_ref, v_ref, start_ref, out_ref, total_ref):
    for first in range(0, q_ref.shape[0], BLOCK):
        rows, keys = pl.ds(first, BLOCK), first + BLOCK
        scores = dot_nt(q_ref[rows, :], k_ref[:keys, :])
        scores = jnp.where(allowed_keys(start_ref, first, keys), scores, masked_score)
        top = jnp.max(scores, axis=1, keepdims=True)
        raw = jnp.exp(scores - top)
        total = jnp.sum(raw, axis=1, keepdims=True)
        attended = dot_nn(raw.astype(bf16), v_ref[:keys, :]) / total
        out_ref[rows, :] = attended.astype(bf16)
        total_ref[rows, :] = top + jnp.log(total)


def attend_back_kernel(
    q_ref, k_ref, v_ref, start_ref, out_ref, grad_ref, total_ref, dq_ref, dk_ref, dv_ref
):
    dk_ref[...] = jnp.zeros_like(dk_ref)
    dv_ref[...] = jnp.zeros_like(dv_ref)
    for first in range(0, q_ref.shape[0], BLOCK):
        rows, keys = pl.ds(first, BLOCK), first + BLOCK
        query, grad = q_ref[rows, :], grad_ref[rows, :]
        key, value = k_ref[:keys, :], v_ref[:keys, :]
        scores = dot_nt(query, key)
        allowed = allowed_keys(start_ref, first, keys)
        prob = jnp.where(allowed, jnp.exp(scores - total_ref[rows, :]), 0.0)
        delta = jnp.sum(grad.astype(f32) * out_ref[rows, :].astype(f32), axis=1, keepdims=True)
        score_grad = (prob * (dot_nt(grad, value) - delta)).astype(bf16)
        dq_ref[rows, :] = dot_nn(score_grad, key) * HEAD**-0.5
        dk_ref[:keys, :] += dot_tn(score_grad, query)
        dv_ref[:keys, :] += dot_tn(prob.astype(bf16), grad)


VMEM_LIMIT = 48 * 1024 * 1024


def attend(queries, keys_all, values_all, starts):
    rows = queries.shape[0]
    return pl.pallas_call(
        attend_kernel,
        out_shape=(
            jax.ShapeDtypeStruct((rows, HEAD), bf16),
            jax.ShapeDtypeStruct((rows, 1), f32),
        ),
        compiler_params=pltpu.CompilerParams(vmem_limit_bytes=VMEM_LIMIT),
        cost_estimate=pl.CostEstimate(
            flops=2 * rows * rows * HEAD, bytes_accessed=rows * 1024, transcendentals=rows * rows // 2
        ),
        name="attend",
    )(queries, keys_all, values_all, starts)


def attend_back(queries, keys_all, values_all, starts, attended, attended_grad, totals):
    rows = queries.shape[0]
    return pl.pallas_call(
        attend_back_kernel,
        out_shape=(jax.ShapeDtypeStruct((rows, HEAD), f32),) * 3,
        compiler_params=pltpu.CompilerParams(vmem_limit_bytes=VMEM_LIMIT),
        cost_estimate=pl.CostEstimate(
            flops=5 * rows * rows * HEAD, bytes_accessed=rows * 4096, transcendentals=rows * rows // 2
        ),
        name="attend_back",
    )(queries, keys_all, values_all, starts, attended, attended_grad, totals)


def rotary_tables(places):
    half_rot = ROT // 2
    inverse = 1.0 / 10000.0 ** (jnp.arange(half_rot, dtype=f32) * (2.0 / ROT))
    angles = inverse[:, None] * places.astype(f32)[None, :]
    return (jnp.cos(angles).T, jnp.sin(angles).T)


def rotate(values, cosine, sine):
    half_rot = ROT // 2
    lower_half = values[..., :half_rot]
    upper_half = values[..., half_rot:ROT]
    return jnp.concatenate(
        [
            lower_half * cosine - upper_half * sine,
            upper_half * cosine + lower_half * sine,
            values[..., ROT:],
        ],
        axis=-1,
    )


def gelu_tanh(values):
    return jax.nn.gelu(values, approximate=True)


def adam_step(value, gradient, first_state, second_state):
    first_new = beta_first * first_state + (1.0 - beta_first) * gradient
    second_new = beta_second * second_state + (1.0 - beta_second) * gradient * gradient
    corrected = first_new / (1.0 - beta_first**STEP)
    root_term = jnp.sqrt(second_new / (1.0 - beta_second**STEP)) + adam_floor
    return (first_new, second_new, value - rate_vector * corrected / root_term)


def gather_row(x):
    return lax.all_gather(x, "row", axis=0, tiled=True)


def swap_col(x):
    return lax.all_to_all(x, "col", split_axis=0, concat_axis=0, tiled=True)


def sum_scatter(x, axis):
    return lax.psum_scatter(x, axis, scatter_dimension=0, tiled=True)


def take_rows(x, index):
    return x.at[index].get(mode="promise_in_bounds")


def high_low(x):
    high_part = x.astype(bf16)
    return high_part, (x - high_part.astype(f32)).astype(bf16)


def per_device(
    tokens,
    cotangent,
    lengths,
    deal_order,
    qkv_weight,
    up_weight,
    proj_weight,
    down_weight,
    norm_vectors,
    qkv_bias,
    mlp_bias,
    qkv_momentum,
    up_momentum,
    proj_momentum,
    down_momentum,
    norm_moment,
    norm_square,
    qkv_bias_moment,
    qkv_bias_square,
    mlp_bias_moment,
    mlp_bias_square,
):
    cols, rows = lax.axis_size("col"), lax.axis_size("row")
    col, row = lax.axis_index("col"), lax.axis_index("row")
    total_tokens = deal_order.shape[0]
    group = total_tokens // cols
    piece = group // rows
    held = total_tokens // rows
    feats = D // cols
    qkv_width, up_width = qkv_weight.shape[1], up_weight.shape[1]
    proj_width = proj_weight.shape[0]
    in_width = qkv_width + up_width
    out_width = proj_width + down_weight.shape[0]

    seq_ends = jnp.cumsum(lengths)
    seq_starts = seq_ends - lengths
    anchor = lax.dynamic_slice_in_dim(deal_order, col * group, group)
    before = seq_ends[None, :] <= anchor[:, None]
    places = anchor - jnp.sum(jnp.where(before, lengths[None, :], 0), axis=1)
    starts = (jnp.arange(group, dtype=jnp.int32) - places)[:, None]
    at = jnp.arange(total_tokens, dtype=jnp.int32)
    dealt_starts = jnp.sum(
        jnp.where(deal_order[None, :] == seq_starts[:, None], at[None, :], 0), axis=1
    )
    own = row * held + jnp.arange(held, dtype=jnp.int32)
    holds = (seq_starts[None, :] <= own[:, None]) & (own[:, None] < seq_ends[None, :])
    dealt_at = own + jnp.sum(jnp.where(holds, (dealt_starts - seq_starts)[None, :], 0), axis=1)
    cosine, sine = rotary_tables(places)

    in_weight = jnp.concatenate([qkv_weight, up_weight], axis=1)
    out_weight = jnp.concatenate([proj_weight, down_weight], axis=0)
    vector_parts = []
    rest = norm_vectors
    for _ in range(3):
        vector_parts.append(rest.astype(bf16))
        rest = rest - vector_parts[-1].astype(f32)
    vector_columns = jnp.pad(jnp.concatenate(vector_parts, axis=0).T, ((0, 0), (0, 128 - 9)))
    weight_all = lax.all_gather(
        jnp.concatenate(
            [in_weight.astype(bf16), out_weight.astype(bf16).T, vector_columns], axis=1
        ),
        "col",
        axis=0,
        tiled=True,
    )
    in_all, out_all = weight_all[:, :in_width], weight_all[:, in_width : in_width + out_width]
    vectors_all = weight_all[:, in_width + out_width :].astype(f32).T
    norm_all = vectors_all[0:3] + vectors_all[3:6] + vectors_all[6:9]

    pick = lax.dynamic_slice(
        deal_order.reshape(cols, rows, piece), (0, row, 0), (cols, 1, piece)
    ).reshape(-1)

    def deal(x):
        mine = take_rows(gather_row(x), pick).reshape(cols, piece, feats)
        return swap_col(mine).transpose(1, 0, 2).reshape(piece, D)

    def deal_back(x, more, own_more):
        parts = x.astype(bf16).reshape(piece, cols, feats).transpose(1, 0, 2)
        if more is None:
            stride = piece
            swapped = swap_col(parts)
        else:
            stride = piece + EXTRA
            swapped = swap_col(jnp.concatenate([parts, more], axis=1))
            own_more = jnp.pad(
                own_more[None], ((0, cols - 1), (stride - own_more.shape[0], 0), (0, 0))
            )
            swapped = swapped + own_more
        whole = gather_row(swapped.reshape(cols * stride, feats))
        block, inside = dealt_at // group, dealt_at % group
        index = (inside // piece) * (cols * stride) + block * stride + inside % piece
        return take_rows(whole, index), whole

    gain, shift, out_bias = norm_vectors[0], norm_vectors[1], norm_vectors[2]
    piece_tokens = deal(tokens).astype(f32)
    centered = piece_tokens - jnp.mean(piece_tokens, axis=1, keepdims=True)
    inverse_std = lax.rsqrt(jnp.mean(centered * centered, axis=1, keepdims=True) + norm_floor)
    normalized = centered * inverse_std
    normed = (normalized * norm_all[0] + norm_all[1]).astype(bf16)
    dealt = gather_row(normed)
    cotangent_dealt = gather_row(deal(cotangent))

    preact = dot_nn(dealt, in_all)
    pre_qkv = preact[:, :qkv_width] + qkv_bias
    pre_up = preact[:, qkv_width:] + mlp_bias
    queries = (rotate(pre_qkv[:, :HEAD], cosine, sine).astype(bf16) * HEAD**-0.5).astype(bf16)
    keys_all = rotate(pre_qkv[:, HEAD : 2 * HEAD], cosine, sine).astype(bf16)
    values_all = pre_qkv[:, 2 * HEAD :].astype(bf16)
    attended, totals = attend(queries, keys_all, values_all, starts)
    activated, gelu_back = jax.vjp(gelu_tanh, pre_up)
    branch = jnp.concatenate([attended, activated.astype(bf16)], axis=1)
    branch_sum = sum_scatter(dot_nt(branch, out_all).astype(bf16), "row")
    branch_back, _ = deal_back(branch_sum, None, None)
    output = tokens.astype(f32) + branch_back.astype(f32) + out_bias

    branch_grad = dot_nn(cotangent_dealt, out_all)
    out_grad = sum_scatter(dot_tn(cotangent_dealt, branch), "col")
    attended_grad = branch_grad[:, :proj_width].astype(bf16)
    up_pre_grad = gelu_back(branch_grad[:, proj_width:])[0]
    query_grad, key_grad, value_grad = attend_back(
        queries, keys_all, values_all, starts, attended, attended_grad, totals
    )
    preact_grad = jnp.concatenate(
        [
            rotate(query_grad, cosine, -sine),
            rotate(key_grad, cosine, -sine),
            value_grad,
            up_pre_grad,
        ],
        axis=1,
    ).astype(bf16)
    in_part = dot_tn(dealt, preact_grad).reshape(cols, feats, in_width)
    bias_part = jnp.sum(preact_grad, axis=0, dtype=f32)
    bias_rows = jnp.broadcast_to(bias_part[None, None, :], (cols, 8, in_width))
    in_sum = sum_scatter(
        jnp.concatenate([in_part, bias_rows], axis=1).reshape(cols * (feats + 8), in_width), "col"
    )
    in_grad, in_bias_grad = in_sum[:feats], in_sum[feats]
    normed_grad = sum_scatter(dot_nt(preact_grad, in_all).astype(bf16), "row").astype(f32)
    scaled = normed_grad * norm_all[0]
    mean_first = jnp.mean(scaled, axis=1, keepdims=True)
    mean_second = jnp.mean(scaled * normalized, axis=1, keepdims=True)
    token_grad = inverse_std * (scaled - mean_first - normalized * mean_second)
    vector_rows = jnp.stack(
        [
            *high_low(jnp.sum(normed_grad * normalized, axis=0)),
            *high_low(jnp.sum(normed_grad, axis=0)),
        ],
        axis=0,
    )
    vector_rows = jnp.pad(
        vector_rows.reshape(4, cols, feats).transpose(1, 0, 2), ((0, 0), (0, EXTRA - 4), (0, 0))
    )
    bias_rows = jnp.stack(high_low(jnp.sum(cotangent, axis=0, dtype=f32)), axis=0)
    token_back, whole = deal_back(token_grad, vector_rows, bias_rows)
    input_grad = cotangent.astype(f32) + token_back.astype(f32)
    vector_sum = jnp.sum(
        whole.reshape(rows * cols, piece + EXTRA, feats)[:, piece:].astype(f32), axis=0
    )
    norm_grads = jnp.stack(
        [
            vector_sum[0] + vector_sum[1],
            vector_sum[2] + vector_sum[3],
            vector_sum[-2] + vector_sum[-1],
        ],
        axis=0,
    )

    flip_flags = (False, False, True, True)
    oriented_grads = (
        in_grad[:, :qkv_width],
        in_grad[:, qkv_width:],
        out_grad[:, :proj_width],
        out_grad[:, proj_width:],
    )
    gradients = [g.T if f else g for g, f in zip(oriented_grads, flip_flags)]
    old_states = (qkv_momentum, up_momentum, proj_momentum, down_momentum)
    weights = (qkv_weight, up_weight, proj_weight, down_weight)
    widths = (3 * D, FF, D, FF)
    states = [momentum * old + g for old, g in zip(old_states, gradients)]
    oriented = []
    for gradient, state, flipped in zip(gradients, states, flip_flags):
        direction = gradient + momentum * state
        direction = direction.T if flipped else direction
        direction = jnp.pad(direction, ((0, 0), (0, up_width - direction.shape[1])))
        oriented += [direction, direction]
    matrix = swap_col(jnp.stack(oriented, axis=0)).reshape(D, up_width)
    gram = lax.psum(dot_nt(matrix, matrix, precision=high), "row")
    shrink = 1.0 / (jnp.sqrt(jnp.trace(gram)) + ortho_floor)
    half = up_width // 2
    thin = lax.dynamic_slice_in_dim(matrix, (col % 2) * half, half, axis=1) * shrink
    gram = gram * (shrink * shrink)
    eye = jnp.eye(D, dtype=f32)
    for sweep in range(5):
        squared = dot_nn(gram, gram, precision=high)
        poly = poly_linear * eye + poly_square * gram + poly_cubic * squared
        thin = dot_nn(poly, thin, precision=high)
        if sweep < 4:
            gram = dot_nn(gram, dot_nn(poly, poly, precision=high), precision=high)
    returned = swap_col(thin.astype(bf16).reshape(cols, feats, half))
    new_weights = []
    for index in range(4):
        update = jnp.concatenate([returned[2 * index], returned[2 * index + 1]], axis=1)
        update = update[:, : oriented_grads[index].shape[1]].astype(f32)
        update = update.T if flip_flags[index] else update
        new_weights.append(
            weights[index] * (1.0 - rate_matrix * decay_matrix)
            - rate_matrix * 0.2 * math.sqrt(widths[index]) * update
        )

    norm_first, norm_second, norm_new = adam_step(
        norm_vectors, norm_grads, norm_moment, norm_square
    )
    qkv_first, qkv_second, qkv_bias_new = adam_step(
        qkv_bias, in_bias_grad[:qkv_width], qkv_bias_moment, qkv_bias_square
    )
    mlp_first, mlp_second, mlp_bias_new = adam_step(
        mlp_bias, in_bias_grad[qkv_width:], mlp_bias_moment, mlp_bias_square
    )
    return (
        output,
        input_grad,
        *gradients,
        *states,
        *new_weights,
        norm_first,
        norm_second,
        norm_new,
        qkv_first,
        qkv_second,
        qkv_bias_new,
        mlp_first,
        mlp_second,
        mlp_bias_new,
    )


def solution(mesh):
    over_both, over_flip = P("row", "col"), P("col", "row")
    features, hidden = P(None, "col"), P("row")
    return jax.shard_map(
        per_device,
        mesh=mesh,
        in_specs=(
            *(over_both, over_both, P(), P()),
            *(over_flip, over_flip, over_both, over_both),
            *(features, hidden, hidden),
            *(over_flip, over_flip, over_both, over_both),
            *(features, features, hidden, hidden, hidden, hidden),
        ),
        out_specs=(
            *(over_both, over_both),
            *(over_flip, over_flip, over_both, over_both) * 3,
            *(features,) * 3,
            *(hidden,) * 6,
        ),
        check_vma=False,
    )
```

time: 2010 us -> 897 us (0.45)
  waiting for transfers between devices: 1250 us -> 534 us
  local copies, waits for them, and re-layouts: 408 us -> 74.7 us
  blocking collectives: 95.7 us -> 37.4 us
  matrix products: 166 us -> 141 us
    psum x5 -> x1, waiting for transfers between devices: 518 us -> 137 us  [per_device(): gram = lax.psum(dot_nt(matrix, matrix, precision=high), 'row')]
    reduce_scatter x4 -> x3, waiting for transfers between devices: 490 us -> 132 us  [sum_scatter(): return lax.psum_scatter(x, axis, scatter_dimension=0, tiled=True)]
    gather x4, local copies, waits for them, and re-layouts: 260 us -> 23.8 us  [take_rows(): return x.at[index].get(mode='promise_in_bounds')]
    psum x3 -> x0, blocking collectives: 77.3 us -> none  [the longest x1 38.1 us: per_device(): lax.psum((jnp.sum(normed_grad * normalized, axis=0), jnp.sum(normed_grad,...]
    scatter x1 -> x0, local copies, waits for them, and re-layouts: 60.8 us -> none  [per_device(): jnp.zeros_like(deal_order).at[deal_order]]
    all_gather x2 -> x0, local copies, waits for them, and re-layouts: 36.4 us -> none  [the longest x1 20.2 us: per_device(): preact_grad_all = lax.all_gather(preact_grad, 'col', axis=0, tiled=True)]
    dot_general x49 -> x24, matrix products: 166 us -> 137 us  [the longest x20 117 us: dot_nn(): lax.dot_general(a, b, (((1,), (0,)), ((), ())), preferred_element_type=f3...]
    unnamed x13, waiting for transfers between devices: 0.89 us -> 26.6 us
  transfers between devices with their start and end apart: 14 -> 15, of which waited for: 10 -> 12; matrix products, arithmetic and copies ran while one was open for 27% -> 26% of each run, Pallas kernels for 0% -> 1%
where the time goes in v1:
time: 897 us; the launch traced here: 890 us
  waiting for transfers between devices  534 us (60%)
  matrix products  141 us (16%)
  local copies, waits for them, and re-layouts  74.7 us (8%)
  other arithmetic  57.9 us (6%)
  blocking collectives  37.4 us (4%)
  between operations  16.3 us (2%)
  Pallas kernels  14.9 us (2%)
  starting transfers between devices  14.1 us (2%)
    all_gather x6, waiting for transfers between devices, gather_row(): return lax.all_gather(x, 'row', axis=0, tiled=True)  177 us
    psum x1, waiting for transfers between devices, per_device(): gram = lax.psum(dot_nt(matrix, matrix, precision=high), 'row')  137 us
    reduce_scatter x3, waiting for transfers between devices, sum_scatter(): return lax.psum_scatter(x, axis, scatter_dimension=0, tiled=True)  132 us
    dot_general x20, matrix products, dot_nn(): lax.dot_general(a, b, (((1,), (0,)), ((), ())), preferred_element_type=f3...  117 us
    all_gather x1, waiting for transfers between devices, per_device(): lax.all_gather(jnp.concatenate([in_weight.astype(bf16), out_weight.astype...  43.2 us
    all_to_all x3, blocking collectives, swap_col(): return lax.all_to_all(x, 'col', split_axis=0, concat_axis=0, tiled=True)  37.4 us
    unnamed x13, waiting for transfers between devices  26.6 us
    gather x4, local copies, waits for them, and re-layouts, take_rows(): return x.at[index].get(mode='promise_in_bounds')  23.8 us
  transfers between devices with their start and end apart: 15, of which 12 were waited for; matrix products, arithmetic and copies ran while one was open for 26% of the time, Pallas kernels for 1%

profile of v1, /device:TPU:0, one launch (start us, length us, event | category | flops | bytes accessed | tf_op | source)
XLA Modules:
  0.0 889.7 jit_solution(3934495376828807291)
XLA Ops:
  14.6 43.2 %all-gather.10.cloned.1.call-done = bf16[1024,896]{0,1:T(8,128)(2,1)} async-done(((bf16[128,896]{0,1:T(8,128)(2,1)}), bf16[1024,896]{0,1:T(8,128)(2,1)}) %all-gather.10.cloned.1.call-update) | async-done | bytes 1835024 | tf_op jit(solution)/shard_map/all_gather | solution.py:232
  58.9 58.4 %all-gather.8.cloned.1.call-done = bf16[16384,128]{1,0:T(8,128)(2,1)} async-done(((bf16[1024,128]{1,0:T(8,128)(2,1)}), bf16[16384,128]{1,0:T(8,128)(2,1)}) %all-gather.8.cloned.1.call-update) | async-done | bytes 4194320 | tf_op jit(solution)/shard_map/all_gather | solution.py:154
  128.4 7.6 all-to-all-done
  137.5 37.3 %all-gather.16.cloned.1.call-done = bf16[16384,128]{1,0:T(8,128)(2,1)} async-done(((bf16[1024,128]{1,0:T(8,128)(2,1)}), bf16[16384,128]{1,0:T(8,128)(2,1)}) %all-gather.16.cloned.1.call-update) | async-done | bytes 4194320 | tf_op jit(solution)/shard_map/all_gather | solution.py:154
  180.6 11.9 %all_to_all.30 = bf16[8,128,128]{1,2,0:T(8,128)(2,1)} all-to-all(bf16[8,128,128]{1,2,0:T(8,128)(2,1)S(1)} %copy.170), channel_id=1, replica_groups=mesh['row'=16,'col'=8] {'col'}, dimensions={0} | all-to-all | bytes 524288 | tf_op jit(solution)/shard_map/all_to_all | solution.py:158
  195.8 35.6 %all-gather.12.cloned.1.call-done = bf16[2048,1024]{1,0:T(8,128)(2,1)} async-done(((bf16[128,1024]{1,0:T(8,128)(2,1)}), bf16[2048,1024]{1,0:T(8,128)(2,1)}) %all-gather.12.cloned.1.call-update) | async-done | bytes 4194320 | tf_op jit(solution)/shard_map/all_gather | solution.py:154
  242.9 45.3 %all-gather.18.cloned.1.call-done = bf16[2048,1024]{0,1:T(8,128)(2,1)} async-done(((bf16[128,1024]{0,1:T(8,128)(2,1)}), bf16[2048,1024]{0,1:T(8,128)(2,1)}) %all-gather.18.cloned.1.call-update) | async-done | bytes 4194320 | tf_op jit(solution)/shard_map/all_gather | solution.py:154
  321.8 9.3 %attend_back.1 = (f32[2048,64]{1,0:T(8,128)S(1)}, f32[2048,64]{1,0:T(8,128)S(1)}, f32[2048,64]{1,0:T(8,128)S(1)}) custom-call(bf16[2048,64]{1,0:T(8,128)(2,1)S(1)} %copy-done.7, bf16[2048,64]{1,0:T(8,128)(2,1)S(1)} %copy-done.9, bf16[2048,64]{1,0:T(8,128)(2,1)S(1)} %copy-done.5, s32[2048,1]{1,0:T(8,128)} %copy-done, bf16[2048,64]{1,0:T(8,128)(2,1)S(1)} %copy-done.3, ...), custom_call_target="tpu_custom_call" | custom-call | flops 1342177280 | bytes 8388608 | tf_op jit(solution)/shard_map/attend_back/pallas_call | solution.py:109
  334.0 7.3 fusion.41
  394.4 25.1 %reduce-scatter.13.cloned.1.call-done = f32[136,448]{1,0:T(8,128)} async-done(((f32[1088,448]{1,0:T(8,128)}), f32[136,448]{1,0:T(8,128)}) %reduce-scatter.13.cloned.1.call-update) | async-done | bytes 243728
  423.5 14.0 %all_to_all.31 = f32[8,128,256]{1,2,0:T(8,128)S(1)} all-to-all(f32[8,128,256]{1,2,0:T(8,128)S(1)} %bitcast_dynamic-update-slice_fusion.1), channel_id=1, replica_groups=mesh['row'=16,'col'=8] {'col'}, dimensions={0} | all-to-all | bytes 2097152 | tf_op jit(solution)/shard_map/all_to_all | solution.py:158
  441.8 61.7 %reduce-scatter.7.cloned.1.call-done = bf16[128,1024]{1,0:T(8,128)(2,1)} async-done(((bf16[2048,1024]{1,0:T(8,128)(2,1)}), bf16[128,1024]{1,0:T(8,128)(2,1)}) %reduce-scatter.7.cloned.1.call-update) | async-done | bytes 262160 | tf_op jit(solution)/shard_map/reduce_scatter | solution.py:162
  504.5 11.5 %all_to_all.32 = bf16[8,128,128]{2,1,0:T(8,128)(2,1)} all-to-all(bf16[8,128,128]{2,1,0:T(8,128)(2,1)S(1)} %bitcast_bitcast_fusion.1), channel_id=1, replica_groups=mesh['row'=16,'col'=8] {'col'}, dimensions={0} | all-to-all | bytes 524288 | tf_op jit(solution)/shard_map/all_to_all | solution.py:158
  517.1 70.0 %reduce-scatter.9.cloned.1.call-done = bf16[128,1024]{1,0:T(8,128)(2,1)} async-done(((bf16[2048,1024]{1,0:T(8,128)(2,1)}), bf16[128,1024]{1,0:T(8,128)(2,1)}) %reduce-scatter.9.cloned.1.call-update) | async-done | bytes 262160 | tf_op jit(solution)/shard_map/reduce_scatter | solution.py:162
  603.0 136.8 %all-reduce.7.cloned.1.call-done = f32[1024,1024]{1,0:T(8,128)} async-done(((f32[1024,1024]{1,0:T(8,128)}), f32[1024,1024]{1,0:T(8,128)}) %all-reduce.7.cloned.1.call-update) | async-done | bytes 4194320 | tf_op jit(solution)/shard_map/psum | solution.py:363
  743.4 12.5 %fusion = f32[1024,1024]{1,0:T(8,128)S(1)} fusion(f32[1024,1024]{1,0:T(8,128)} %all-reduce.7.cloned.1.call-done, f32[]{:T(128)S(6)} %mul.532), kind=kOutput, calls=%fused_computation.9 | convolution fusion | flops 6450839552 | bytes 8388612 | tf_op jit(solution)/shard_map/dot_general | solution.py:46
  755.9 7.0 fusion.108
  765.1 7.2 fusion.9
  772.4 7.5 fusion.1
  779.8 7.1 fusion.109
  795.7 7.9 fusion.2
  805.4 7.1 fusion.111
  819.4 7.7 fusion.3
  828.9 7.4 fusion.113
  (290 shorter events, 227.1 us)
Async XLA Ops:
  7.2 50.7 %all-gather.10.cloned.1.call-start = ((), (), s32[]{:S(2)}) async-start(), calls=%async_computation.11 | async-start | bytes 2064384 | tf_op jit(solution)/shard_map/all_gather | solution.py:232
  12.4 104.9 %all-gather.8.cloned.1.call-start = ((), (), s32[]{:S(2)}) async-start(), calls=%async_computation.10 | async-start | bytes 4456448 | tf_op jit(solution)/shard_map/all_gather | solution.py:154
  13.1 161.7 %all-gather.16.cloned.1.call-start = ((), (), s32[]{:S(2)}) async-start(), calls=%async_computation.15 | async-start | bytes 4456448 | tf_op jit(solution)/shard_map/all_gather | solution.py:154
  58.9 134.4 %copy-start.49 = (s32[32]{0:T(128)S(1)}, s32[32]{0:T(128)}, u32[]{:S(2)}) copy-start(s32[32]{0:T(128)} %param.23) | copy-start | bytes 388
  58.9 172.5 %copy-start.33 = (bf16[1024,896]{0,1:T(8,128)(2,1)S(1)}, bf16[1024,896]{0,1:T(8,128)(2,1)}, u32[]{:S(2)}) copy-start(bf16[1024,896]{0,1:T(8,128)(2,1)} %all-gather.10.cloned.1.call-done) | copy-start | bytes 5505028
  124.1 12.0 %all-to-all-start = ((bf16[8,128,128]{2,1,0:T(8,128)(2,1)}), bf16[8,128,128]{2,1,0:T(8,128)(2,1)S(1)}, u32[]{:S(2)}, u32[]{:S(2)}) async-start(bf16[8,128,128]{2,1,0:T(8,128)(2,1)} %bitcast.3), calls=%async_computation | async-start | bytes 524288 | tf_op jit(solution)/shard_map/all_to_all | solution.py:158
  128.4 103.1 %all-gather.12.cloned.1.call-start = ((), (), s32[]{:S(2)}) async-start(), calls=%async_computation.12 | async-start | bytes 4456448 | tf_op jit(solution)/shard_map/all_gather | solution.py:154
  137.4 150.7 %all-gather.18.cloned.1.call-start = ((), (), s32[]{:S(2)}) async-start(), calls=%async_computation.16 | async-start | bytes 4456448 | tf_op jit(solution)/shard_map/all_gather | solution.py:154
  192.5 200.5 %reduce-scatter.11.cloned.1.call-start = ((), (), s32[]{:S(2)}) async-start(), calls=%async_computation.19 | async-start | bytes 1474560 | tf_op jit(solution)/shard_map/reduce_scatter | solution.py:162
  195.2 108.9 %copy-start = (s32[2048,1]{1,0:T(8,128)}, s32[2048,1]{1,0:T(8,128)S(1)}, u32[]{:S(2)}) copy-start(s32[2048,1]{1,0:T(8,128)S(1)} %copy.167.start_ref) | copy-start | bytes 24580
  316.0 103.5 %reduce-scatter.13.cloned.1.call-start = ((), (), s32[]{:S(2)}) async-start(), calls=%async_computation.21 | async-start | bytes 2506752
  378.9 124.6 %reduce-scatter.7.cloned.1.call-start = ((), (), s32[]{:S(2)}) async-start(), calls=%async_computation.13 | async-start | bytes 4456448 | tf_op jit(solution)/shard_map/reduce_scatter | solution.py:162
  384.5 202.5 %reduce-scatter.9.cloned.1.call-start = ((), (), s32[]{:S(2)}) async-start(), calls=%async_computation.17 | async-start | bytes 4456448 | tf_op jit(solution)/shard_map/reduce_scatter | solution.py:162
  392.0 347.7 %all-reduce.7.cloned.1.call-start = ((), (), s32[]{:S(2)}) async-start(), calls=%async_computation.20 | async-start | bytes 8388608 | tf_op jit(solution)/shard_map/psum | solution.py:363
  441.7 74.4 %copy-start.41 = (s32[32]{0:T(128)S(1)}, s32[32]{0:T(128)}, u32[]{:S(2)}) copy-start(s32[32]{0:T(128)} %copy-done.40) | copy-start | bytes 388
  441.7 74.4 %copy-start.31 = (s32[16384]{0:T(1024)S(1)}, s32[16384]{0:T(1024)}, u32[]{:S(2)}) copy-start(s32[16384]{0:T(1024)} %param.24) | copy-start | bytes 196612
  441.7 75.0 %copy-start.15 = (bf16[1024,128]{1,0:T(8,128)(2,1)S(1)}, bf16[1024,128]{1,0:T(8,128)(2,1)}, u32[]{:S(2)}) copy-start(bf16[1024,128]{1,0:T(8,128)(2,1)} %param.22) | copy-start | bytes 786436
  441.7 75.2 %copy-start.37 = (f32[3,128]{1,0:T(4,128)S(1)}, f32[3,128]{1,0:T(4,128)}, u32[]{:S(2)}) copy-start(f32[3,128]{1,0:T(4,128)} %param.29) | copy-start | bytes 4612
  441.7 145.3 %copy-start.39 = (f32[128]{0:T(128)S(1)}, f32[128]{0:T(128)}, u32[]{:S(2)}) copy-start(f32[128]{0:T(128)} %copy-done.38) | copy-start | bytes 1540
  441.8 145.3 %copy-start.43 = (f32[128]{0:T(128)S(1)}, f32[128]{0:T(128)}, u32[]{:S(2)}) copy-start(f32[128]{0:T(128)} %copy-done.42) | copy-start | bytes 1540
  441.8 425.9 %all-gather.14.cloned.1.call-start = ((), (), s32[]{:S(2)}) async-start(), calls=%async_computation.14 | async-start | bytes 4456448 | tf_op jit(solution)/shard_map/all_gather | solution.py:154
  590.3 11.9 %all-to-all-start.3 = ((bf16[8,144,128]{2,1,0:T(8,128)(2,1)}), bf16[8,144,128]{2,1,0:T(8,128)(2,1)S(1)}, u32[]{:S(2)}, u32[]{:S(2)}) async-start(bf16[8,144,128]{2,1,0:T(8,128)(2,1)} %fusion.80), calls=%async_computation.5 | async-start | bytes 589824 | tf_op jit(solution)/shard_map/all_to_all | solution.py:158
  594.7 279.5 %all-gather.20.cloned.1.call-start = ((), (), s32[]{:S(2)}) async-start(), calls=%async_computation.18 | async-start | bytes 5013504 | tf_op jit(solution)/shard_map/all_gather | solution.py:154
  853.3 11.6 %all-to-all-start.5 = ((bf16[8,128,128]{1,2,0:T(8,128)(2,1)}), bf16[8,128,128]{1,2,0:T(8,128)(2,1)S(1)}, u32[]{:S(2)}, u32[]{:S(2)}) async-start(bf16[8,128,128]{1,2,0:T(8,128)(2,1)} %copy.189), calls=%async_computation.8 | async-start | bytes 524288 | tf_op jit(solution)/shard_map/all_to_all | solution.py:158
  (47 other events, 667.9 us)
Sparse Core Ops, SparseCore 0:
  12.5 45.3 all-gather.9
  60.3 56.8 all-gather.7
  119.7 54.9 all-gather.15
  177.7 53.7 all-gather.11
  233.5 54.5 all-gather.17
  316.1 37.2 reduce-scatter.10
  379.0 40.4 reduce-scatter.12
  424.0 79.4 reduce-scatter.6
  507.6 79.4 reduce-scatter.8
  589.6 150.1 all-reduce.6
  742.5 56.0 all-gather.13
  801.8 55.4 all-gather.19

commit v2 on v1

--- a/solution.py
+++ b/solution.py
@@ -27,7 +27,6 @@
 norm_floor = 1e-05
 ortho_floor = 1e-07
 masked_score = -1e30
-high = lax.Precision.HIGH
 f32 = jnp.float32
 bf16 = jnp.bfloat16
 BLOCK = 256
@@ -86,6 +85,592 @@
 
 
 VMEM_LIMIT = 48 * 1024 * 1024
+
+
+MESH = pl.DeviceIdType.MESH
+VMEM_SPEC = pl.BlockSpec(memory_space=pltpu.VMEM)
+SMEM_SPEC = pl.BlockSpec(memory_space=pltpu.SMEM)
+
+
+def remote(src, dst, send, recv, device):
+    return pltpu.make_async_remote_copy(
+        src_ref=src, dst_ref=dst, send_sem=send, recv_sem=recv, device_id=device, device_id_type=MESH
+    )
+
+
+class Place:
+    def __init__(self):
+        self.row, self.col = lax.axis_index("row"), lax.axis_index("col")
+        self.rows, self.cols = lax.axis_size("row"), lax.axis_size("col")
+        self.chips = self.rows // 2
+        self.chip, self.core = self.row // 2, self.row % 2
+        self.twin = (self.chip * 2 + 1 - self.core, self.col)
+
+    def chip_at(self, step):
+        return lax.rem(self.chip + step, self.chips)
+
+    def chip_row(self, step):
+        return self.chip_at(step) * 2 + self.core
+
+    def col_at(self, step):
+        return lax.rem(self.col + step, self.cols)
+
+
+def meet(devices):
+    barrier = pltpu.get_barrier_semaphore()
+    for device in devices:
+        pl.semaphore_signal(barrier, inc=1, device_id=device, device_id_type=MESH)
+    pl.semaphore_wait(barrier, len(devices))
+
+
+class RowGather:
+    def __init__(self, at, slot, sems):
+        self.at, self.slot = at, slot
+        self.send, self.recv, self.pass_send, self.pass_recv = sems
+
+    def outgoing(self, step, src):
+        at = self.at
+        return remote(
+            src,
+            self.slot(at.row),
+            self.send.at[step],
+            self.recv.at[step],
+            (at.chip_row(step), at.col),
+        )
+
+    def passing(self, step, src, row):
+        return remote(
+            src, self.slot(row), self.pass_send.at[step], self.pass_recv.at[step], self.at.twin
+        )
+
+    def came_from(self, step):
+        return self.at.chip_row(self.at.chips - step)
+
+    def start(self, src):
+        self.src = src
+        for step in range(1, self.at.chips):
+            self.outgoing(step, src).start()
+        self.passing(0, src, self.at.row).start()
+
+    def forward(self, then=None):
+        for step in range(1, self.at.chips):
+            row = self.came_from(step)
+            slot = self.slot(row)
+            remote(
+                slot, slot, self.send.at[step], self.recv.at[step], (row, self.at.col)
+            ).wait_recv()
+            self.passing(step, slot, row).start()
+            if then is not None:
+                then(row)
+
+    def finish(self, then=None):
+        at = self.at
+        for step in range(at.chips):
+            row = at.chip_at(at.chips - step) * 2 + 1 - at.core
+            slot = self.slot(row)
+            remote(
+                slot, slot, self.pass_send.at[step], self.pass_recv.at[step], at.twin
+            ).wait_recv()
+            if then is not None:
+                then(row)
+
+    def sent(self):
+        for step in range(1, self.at.chips):
+            self.outgoing(step, self.src).wait_send()
+        self.passing(0, self.src, self.at.row).wait_send()
+        for step in range(1, self.at.chips):
+            row = self.came_from(step)
+            self.passing(step, self.slot(row), row).wait_send()
+
+
+class ColSwap:
+    def __init__(self, at, src, dst, sems):
+        self.at, self.src, self.dst = at, src, dst
+        self.send, self.recv = sems
+
+    def outgoing(self, step):
+        at = self.at
+        to = at.col_at(step)
+        return remote(
+            self.src(to), self.dst(at.col), self.send.at[step], self.recv.at[step], (at.row, to)
+        )
+
+    def start(self):
+        for step in range(1, self.at.cols):
+            self.outgoing(step).start()
+
+    def arrived(self):
+        at = self.at
+        for step in range(1, at.cols):
+            came = at.col_at(at.cols - step)
+            slot = self.dst(came)
+            remote(slot, slot, self.send.at[step], self.recv.at[step], (at.row, came)).wait_recv()
+
+    def sent(self):
+        for step in range(1, self.at.cols):
+            self.outgoing(step).wait_send()
+
+
+def gather_sems(chips):
+    return [pltpu.SemaphoreType.DMA((chips,))] * 4
+
+
+def swap_sems(cols):
+    return [pltpu.SemaphoreType.DMA((cols,))] * 2
+
+
+def deal_kernel(
+    tokens_ref,
+    cotangent_ref,
+    pick_ref,
+    weight_ref,
+    vector_ref,
+    dealt_ref,
+    cot_dealt_ref,
+    weight_all_ref,
+    vector_all_ref,
+    normalized_ref,
+    inverse_std_ref,
+    all_tokens,
+    all_cots,
+    wide,
+    chosen,
+    out_tokens,
+    in_tokens,
+    out_cots,
+    in_cots,
+    *sems,
+):
+    at = Place()
+    held, feats = tokens_ref.shape
+    piece = out_tokens.shape[1]
+    depth = weight_ref.shape[0]
+    sems = list(sems)
+
+    def some(count):
+        taken, sems[:count] = sems[:count], []
+        return taken
+
+    def dealt_slot(ref):
+        return lambda row: ref.at[pl.ds(row * piece, piece), :]
+
+    first_tokens = RowGather(at, lambda row: all_tokens.at[row], some(4))
+    first_cots = RowGather(at, lambda row: all_cots.at[row], some(4))
+    last_tokens = RowGather(at, dealt_slot(dealt_ref), some(4))
+    last_cots = RowGather(at, dealt_slot(cot_dealt_ref), some(4))
+    swap_tokens = ColSwap(at, lambda c: out_tokens.at[c], lambda c: in_tokens.at[c], some(2))
+    swap_cots = ColSwap(at, lambda c: out_cots.at[c], lambda c: in_cots.at[c], some(2))
+    swap_weight = ColSwap(
+        at, lambda c: weight_ref, lambda c: weight_all_ref.at[pl.ds(c * depth, depth), :], some(2)
+    )
+    swap_vector = ColSwap(at, lambda c: vector_ref, lambda c: vector_all_ref.at[c], some(2))
+
+    meet(
+        [(at.chip_row(step), at.col) for step in range(1, at.chips)]
+        + [at.twin]
+        + [(at.row, at.col_at(step)) for step in range(1, at.cols)]
+    )
+    first_tokens.start(tokens_ref)
+    swap_vector.start()
+    swap_weight.start()
+    weight_all_ref[pl.ds(at.col * depth, depth), :] = weight_ref[...]
+    vector_all_ref[at.col] = vector_ref[...]
+
+    def widen(src):
+        def one(row):
+            wide[pl.ds(row * held, held), :] = src[row].astype(f32)
+
+        return one
+
+    def choose(out_ref):
+        def eight(step, carry):
+            first = step * 8
+            found = [wide[pl.ds(pick_ref[first + i], 1), :] for i in range(8)]
+            chosen[pl.ds(first, 8), :] = jnp.concatenate(found, axis=0)
+            return carry
+
+        lax.fori_loop(0, at.cols * piece // 8, eight, 0)
+        for c in range(at.cols):
+            out_ref[c] = chosen[c * piece : (c + 1) * piece, :].astype(bf16)
+
+    wide[pl.ds(at.row * held, held), :] = tokens_ref[...].astype(f32)
+    first_tokens.forward(widen(all_tokens))
+    first_cots.start(cotangent_ref)
+    first_tokens.finish(widen(all_tokens))
+    choose(out_tokens)
+    swap_tokens.start()
+    in_tokens[at.col] = out_tokens[at.col]
+    swap_vector.arrived()
+    swap_tokens.arrived()
+    width = at.cols * feats
+    parts = [in_tokens[f].astype(f32) for f in range(at.cols)]
+    mean = sum(jnp.sum(part, axis=1, keepdims=True) for part in parts) / width
+    parts = [part - mean for part in parts]
+    variance = sum(jnp.sum(part * part, axis=1, keepdims=True) for part in parts) / width
+    inverse_std = lax.rsqrt(variance + norm_floor)
+    inverse_std_ref[...] = inverse_std
+    own = pl.ds(at.row * piece, piece)
+    for f in range(at.cols):
+        lanes = slice(f * feats, (f + 1) * feats)
+        normalized = parts[f] * inverse_std
+        normalized_ref[:, lanes] = normalized
+        vectors = vector_all_ref[f]
+        dealt_ref[own, lanes] = (normalized * vectors[0:1, :] + vectors[1:2, :]).astype(bf16)
+    last_tokens.start(dealt_ref.at[own, :])
+
+    wide[pl.ds(at.row * held, held), :] = cotangent_ref[...].astype(f32)
+    first_cots.forward(widen(all_cots))
+    first_cots.finish(widen(all_cots))
+    choose(out_cots)
+    swap_cots.start()
+    in_cots[at.col] = out_cots[at.col]
+    last_tokens.forward()
+    swap_cots.arrived()
+    for f in range(at.cols):
+        cot_dealt_ref[own, f * feats : (f + 1) * feats] = in_cots[f]
+    last_cots.start(cot_dealt_ref.at[own, :])
+    last_tokens.finish()
+    last_cots.forward()
+    last_cots.finish()
+    swap_weight.arrived()
+    for moved in (first_tokens, first_cots, last_tokens, last_cots):
+        moved.sent()
+    for moved in (swap_tokens, swap_cots, swap_weight, swap_vector):
+        moved.sent()
+
+
+def deal_all(tokens, cotangent, pick, weight, vectors, rows, cols):
+    held, feats = tokens.shape
+    total = held * rows
+    group = total // cols
+    piece = group // rows
+    width = feats * cols
+    chips = rows // 2
+    shape = jax.ShapeDtypeStruct
+    return pl.pallas_call(
+        deal_kernel,
+        out_shape=(
+            shape((group, width), bf16),
+            shape((group, width), bf16),
+            shape((weight.shape[0] * cols, weight.shape[1]), bf16),
+            shape((cols,) + vectors.shape, f32),
+            shape((piece, width), f32),
+            shape((piece, 1), f32),
+        ),
+        in_specs=[VMEM_SPEC, VMEM_SPEC, SMEM_SPEC, VMEM_SPEC, VMEM_SPEC],
+        out_specs=(VMEM_SPEC,) * 6,
+        scratch_shapes=[
+            pltpu.VMEM((rows, held, feats), bf16),
+            pltpu.VMEM((rows, held, feats), bf16),
+            pltpu.VMEM((total, feats), f32),
+            pltpu.VMEM((cols * piece, feats), f32),
+            *([pltpu.VMEM((cols, piece, feats), bf16)] * 4),
+            *(gather_sems(chips) * 4),
+            *(swap_sems(cols) * 4),
+        ],
+        compiler_params=pltpu.CompilerParams(
+            collective_id=0, has_side_effects=True, vmem_limit_bytes=VMEM_LIMIT
+        ),
+        name="deal_all",
+    )(tokens, cotangent, pick, weight, vectors)
+
+
+def split(x):
+    high_part = x.astype(bf16)
+    return high_part, (x - high_part.astype(f32)).astype(bf16)
+
+
+def three(dot, left, right):
+    return dot(left[0], right[0]) + (dot(left[0], right[1]) + dot(left[1], right[0]))
+
+
+BLK = 128
+
+
+def gram_kernel(
+    in_part_ref,
+    bias_ref,
+    out_grad_ref,
+    momentum_ref,
+    in_grad_ref,
+    bias_grad_ref,
+    matrix_ref,
+    gram_ref,
+    parts,
+    biases,
+    chunks,
+    partial,
+    from_twin,
+    half_sum,
+    slices,
+    *sems,
+):
+    at = Place()
+    sems = list(sems)
+
+    def some(count):
+        taken, sems[:count] = sems[:count], []
+        return taken
+
+    swap_part = ColSwap(at, lambda c: in_part_ref.at[c], lambda c: parts.at[c], some(2))
+    swap_bias = ColSwap(at, lambda c: bias_ref, lambda c: biases.at[c], some(2))
+    swap_chunk = ColSwap(at, lambda c: chunks.at[c], lambda c: matrix_ref.at[c], some(2))
+    twin_send, twin_recv, sum_send, sum_recv, all_send, all_recv = some(6)
+    count = at.chips * 2
+    mine = at.chip * 2 + at.col % 2
+    first_col = at.col - at.col % 2
+
+    def member(step):
+        other = lax.rem(mine + step, count)
+        return other, ((other // 2) * 2 + at.core, first_col + other % 2)
+
+    peers = [member(step)[1] for step in range(1, count)]
+    meet([(at.row, at.col_at(step)) for step in range(1, at.cols)] + [at.twin] + peers)
+    swap_part.start()
+    swap_bias.start()
+    parts[at.col] = in_part_ref[at.col]
+    biases[at.col] = bias_ref[...]
+    swap_part.arrived()
+    in_grad = sum(parts[c].astype(f32) for c in range(at.cols))
+    in_grad_ref[...] = in_grad
+    half = in_grad.shape[1] // BLK
+    for index in range(at.cols):
+        lanes = slice(index * BLK, (index + 1) * BLK)
+        if index < half:
+            grad = in_grad[:, lanes]
+        else:
+            grad = out_grad_ref[:, (index - half) * BLK : (index - half + 1) * BLK]
+        state = momentum * momentum_ref[:, lanes] + grad
+        chunks[index] = grad + momentum * state
+    swap_chunk.start()
+    matrix_ref[at.col] = chunks[at.col]
+    swap_bias.arrived()
+    bias_grad_ref[...] = sum(biases[c] for c in range(at.cols))
+    swap_chunk.arrived()
+
+    strips = matrix_ref.shape[0]
+    matrix = split(matrix_ref[...].reshape(strips * BLK, BLK))
+    index = 0
+    for i in range(strips):
+        left = [m[i * BLK : (i + 1) * BLK, :] for m in matrix]
+        right = [m[i * BLK :, :] for m in matrix]
+        product = three(dot_nt, left, right)
+        for j in range(strips - i):
+            partial[index] = product[:, j * BLK : (j + 1) * BLK]
+            index += 1
+    blocks = index // 2
+    to_twin = remote(
+        partial.at[pl.ds((1 - at.core) * blocks, blocks)],
+        from_twin,
+        twin_send.at[0],
+        twin_recv.at[0],
+        at.twin,
+    )
+    to_twin.start()
+    to_twin.wait_recv()
+    for b in range(blocks):
+        half_sum[b * BLK : (b + 1) * BLK, :] = partial[at.core * blocks + b] + from_twin[b]
+
+    size = blocks * BLK // count
+
+    def piece_of(owner):
+        return half_sum.at[pl.ds(owner * size, size), :]
+
+    def give(step):
+        owner, device = member(step)
+        return remote(
+            piece_of(owner), slices.at[mine], sum_send.at[step], sum_recv.at[step], device
+        )
+
+    for step in range(1, count):
+        give(step).start()
+    slices[mine] = half_sum[pl.ds(mine * size, size), :]
+    for step in range(1, count):
+        came, device = member(count - step)
+        remote(
+            slices.at[came], slices.at[came], sum_send.at[step], sum_recv.at[step], device
+        ).wait_recv()
+    total = slices[0]
+    for index in range(1, count):
+        total = total + slices[index]
+    half_rows = blocks * BLK
+
+    def home(owner):
+        return gram_ref.at[pl.ds(at.core * half_rows + owner * size, size), :]
+
+    gram_ref[pl.ds(at.core * half_rows + mine * size, size), :] = total
+
+    def spread(step):
+        return remote(
+            home(mine), home(mine), all_send.at[step], all_recv.at[step], member(step)[1]
+        )
+
+    for step in range(1, count):
+        spread(step).start()
+    for step in range(1, count):
+        came, device = member(count - step)
+        remote(
+            home(came), home(came), all_send.at[step], all_recv.at[step], device
+        ).wait_recv()
+    both = gram_ref.at[pl.ds(at.core * half_rows, half_rows), :]
+    other = gram_ref.at[pl.ds((1 - at.core) * half_rows, half_rows), :]
+    passing = remote(both, both, twin_send.at[1], twin_recv.at[1], at.twin)
+    passing.start()
+    remote(other, other, twin_send.at[1], twin_recv.at[1], at.twin).wait_recv()
+    passing.wait_send()
+    to_twin.wait_send()
+    for step in range(1, count):
+        give(step).wait_send()
+        spread(step).wait_send()
+    for moved in (swap_part, swap_bias, swap_chunk):
+        moved.sent()
+
+
+WIDE = 256
+
+
+def poly_kernel(gram_ref, matrix_ref, out_ref, *buffers):
+    first, second, third, thin = [buffers[2 * i : 2 * i + 2] for i in range(4)]
+    strips = matrix_ref.shape[0]
+    size = strips * BLK
+    counts = range(size // WIDE)
+    eye = lax.broadcasted_iota(jnp.int32, (BLK, BLK), 0) == lax.broadcasted_iota(
+        jnp.int32, (BLK, BLK), 1
+    )
+
+    def put(pair, rows, lanes, value):
+        high_part, low_part = split(value)
+        pair[0][rows, lanes] = high_part
+        pair[1][rows, lanes] = low_part
+
+    def get(pair, rows, lanes):
+        return pair[0][rows, lanes], pair[1][rows, lanes]
+
+    places, index = [], 0
+    for i in range(strips):
+        for j in range(i, strips):
+            places.append((i, j, index))
+            index += 1
+    trace = sum(
+        jnp.sum(jnp.where(eye, gram_ref[at * BLK : (at + 1) * BLK, :], 0.0))
+        for i, j, at in places
+        if i == j
+    )
+    shrink = 1.0 / (jnp.sqrt(jnp.full((1, 1), trace, f32)) + ortho_floor)
+    for i, j, at in places:
+        block = gram_ref[at * BLK : (at + 1) * BLK, :] * (shrink * shrink)
+        here, there = slice(i * BLK, (i + 1) * BLK), slice(j * BLK, (j + 1) * BLK)
+        put(first, here, there, block)
+        if j > i:
+            put(first, there, here, block.T)
+    everything = slice(0, size)
+    for i in range(strips):
+        put(thin, slice(i * BLK, (i + 1) * BLK), everything, matrix_ref[i] * shrink)
+
+    def product(left, right, out, finish=None):
+        for i in counts:
+            rows, rest = slice(i * WIDE, (i + 1) * WIDE), slice(i * WIDE, size)
+            value = three(dot_nn, get(left, rows, everything), get(right, everything, rest))
+            if finish is not None:
+                value = finish(value, rows, rest)
+            put(out, rows, rest, value)
+            for j in range(i + 1, size // WIDE):
+                part = value[:, (j - i) * WIDE : (j - i + 1) * WIDE]
+                put(out, slice(j * WIDE, (j + 1) * WIDE), rows, part.T)
+
+    def thin_product(left):
+        right = get(thin, everything, everything)
+        return [
+            three(dot_nn, get(left, slice(i * WIDE, (i + 1) * WIDE), everything), right)
+            for i in counts
+        ]
+
+    def sweep(gram, poly, square):
+        def finish(value, rows, rest):
+            high_part, low_part = get(gram, rows, rest)
+            value = poly_cubic * value + poly_square * (
+                high_part.astype(f32) + low_part.astype(f32)
+            )
+            at_row = lax.broadcasted_iota(jnp.int32, value.shape, 0)
+            at_lane = lax.broadcasted_iota(jnp.int32, value.shape, 1)
+            return value + jnp.where(at_row == at_lane, poly_linear, 0.0)
+
+        product(gram, gram, poly, finish)
+        for i, value in zip(counts, thin_product(poly)):
+            put(thin, slice(i * WIDE, (i + 1) * WIDE), everything, value)
+        product(poly, poly, square)
+        product(gram, square, poly)
+
+    def two(step, carry):
+        sweep(first, second, third)
+        sweep(second, first, third)
+        return carry
+
+    lax.fori_loop(0, 2, two, 0)
+    once = thin_product(first)
+    old = []
+    for i in counts:
+        rows = slice(i * WIDE, (i + 1) * WIDE)
+        high_part, low_part = get(thin, rows, everything)
+        old.append(high_part.astype(f32) + low_part.astype(f32))
+    for i, value in zip(counts, once):
+        put(thin, slice(i * WIDE, (i + 1) * WIDE), everything, value)
+    for i, value in zip(counts, thin_product(first)):
+        result = poly_linear * old[i] + poly_square * once[i] + poly_cubic * value
+        out_ref[i * WIDE : (i + 1) * WIDE, :] = result.astype(bf16)
+
+
+def orthogonalize(gram, matrix):
+    size, width = matrix.shape[0] * BLK, matrix.shape[2]
+    square, narrow = pltpu.VMEM((size, size), bf16), pltpu.VMEM((size, width), bf16)
+    return pl.pallas_call(
+        poly_kernel,
+        out_shape=jax.ShapeDtypeStruct((size, width), bf16),
+        scratch_shapes=[*([square] * 6), *([narrow] * 2)],
+        compiler_params=pltpu.CompilerParams(vmem_limit_bytes=VMEM_LIMIT),
+        cost_estimate=pl.CostEstimate(
+            flops=48 * size**3, bytes_accessed=12 * size * size, transcendentals=0
+        ),
+        name="orthogonalize",
+    )(gram, matrix)
+
+
+def gram_all(in_part, bias, out_grad, old_momentum, rows, cols):
+    feats, width = in_part.shape[1:]
+    chips = rows // 2
+    blocks = cols * (cols + 1) // 2
+    count = chips * 2
+    half_rows = blocks * BLK // 2
+    shape = jax.ShapeDtypeStruct
+    dma = pltpu.SemaphoreType.DMA
+    return pl.pallas_call(
+        gram_kernel,
+        out_shape=(
+            shape((feats, width), f32),
+            shape(bias.shape, f32),
+            shape((cols, feats, BLK), f32),
+            shape((blocks * BLK, BLK), f32),
+        ),
+        in_specs=[VMEM_SPEC] * 4,
+        out_specs=(VMEM_SPEC,) * 4,
+        scratch_shapes=[
+            pltpu.VMEM((cols, feats, width), bf16),
+            pltpu.VMEM((cols,) + bias.shape, f32),
+            pltpu.VMEM((cols, feats, BLK), f32),
+            pltpu.VMEM((blocks, BLK, BLK), f32),
+            pltpu.VMEM((blocks // 2, BLK, BLK), f32),
+            pltpu.VMEM((half_rows, BLK), f32),
+            pltpu.VMEM((count, half_rows // count, BLK), f32),
+            *(swap_sems(cols) * 3),
+            dma((2,)),
+            dma((2,)),
+            *([dma((count,))] * 4),
+        ],
+        compiler_params=pltpu.CompilerParams(
+            collective_id=1, has_side_effects=True, vmem_limit_bytes=VMEM_LIMIT
+        ),
+        name="gram_all",
+    )(in_part, bias, out_grad, old_momentum)
 
 
 def attend(queries, keys_all, values_all, starts):
@@ -203,8 +788,6 @@
     feats = D // cols
     qkv_width, up_width = qkv_weight.shape[1], up_weight.shape[1]
     proj_width = proj_weight.shape[0]
-    in_width = qkv_width + up_width
-    out_width = proj_width + down_weight.shape[0]
 
     seq_ends = jnp.cumsum(lengths)
     seq_starts = seq_ends - lengths
@@ -221,33 +804,27 @@
     dealt_at = own + jnp.sum(jnp.where(holds, (dealt_starts - seq_starts)[None, :], 0), axis=1)
     cosine, sine = rotary_tables(places)
 
-    in_weight = jnp.concatenate([qkv_weight, up_weight], axis=1)
-    out_weight = jnp.concatenate([proj_weight, down_weight], axis=0)
-    vector_parts = []
-    rest = norm_vectors
-    for _ in range(3):
-        vector_parts.append(rest.astype(bf16))
-        rest = rest - vector_parts[-1].astype(f32)
-    vector_columns = jnp.pad(jnp.concatenate(vector_parts, axis=0).T, ((0, 0), (0, 128 - 9)))
-    weight_all = lax.all_gather(
-        jnp.concatenate(
-            [in_weight.astype(bf16), out_weight.astype(bf16).T, vector_columns], axis=1
-        ),
-        "col",
-        axis=0,
-        tiled=True,
-    )
-    in_all, out_all = weight_all[:, :in_width], weight_all[:, in_width : in_width + out_width]
-    vectors_all = weight_all[:, in_width + out_width :].astype(f32).T
-    norm_all = vectors_all[0:3] + vectors_all[3:6] + vectors_all[6:9]
-
+    def lanes(x, width):
+        return jnp.pad(x, ((0, 0), (0, width - x.shape[1])))
+
+    in_pad = 2 * up_width
+    tile = jnp.concatenate(
+        [
+            lanes(qkv_weight.astype(bf16), up_width),
+            up_weight.astype(bf16),
+            lanes(proj_weight.astype(bf16).T, 128),
+            down_weight.astype(bf16).T,
+        ],
+        axis=1,
+    )
     pick = lax.dynamic_slice(
         deal_order.reshape(cols, rows, piece), (0, row, 0), (cols, 1, piece)
     ).reshape(-1)
-
-    def deal(x):
-        mine = take_rows(gather_row(x), pick).reshape(cols, piece, feats)
-        return swap_col(mine).transpose(1, 0, 2).reshape(piece, D)
+    dealt, cotangent_dealt, weight_all, vector_all, normalized, inverse_std = deal_all(
+        tokens, cotangent, pick, tile, jnp.pad(norm_vectors, ((0, 5), (0, 0))), rows, cols
+    )
+    in_all, out_all = weight_all[:, :in_pad], weight_all[:, in_pad:]
+    gain_all = vector_all[:, 0, :].reshape(1, D)
 
     def deal_back(x, more, own_more):
         parts = x.astype(bf16).reshape(piece, cols, feats).transpose(1, 0, 2)
@@ -266,24 +843,16 @@
         index = (inside // piece) * (cols * stride) + block * stride + inside % piece
         return take_rows(whole, index), whole
 
-    gain, shift, out_bias = norm_vectors[0], norm_vectors[1], norm_vectors[2]
-    piece_tokens = deal(tokens).astype(f32)
-    centered = piece_tokens - jnp.mean(piece_tokens, axis=1, keepdims=True)
-    inverse_std = lax.rsqrt(jnp.mean(centered * centered, axis=1, keepdims=True) + norm_floor)
-    normalized = centered * inverse_std
-    normed = (normalized * norm_all[0] + norm_all[1]).astype(bf16)
-    dealt = gather_row(normed)
-    cotangent_dealt = gather_row(deal(cotangent))
-
+    out_bias = norm_vectors[2]
     preact = dot_nn(dealt, in_all)
     pre_qkv = preact[:, :qkv_width] + qkv_bias
-    pre_up = preact[:, qkv_width:] + mlp_bias
+    pre_up = preact[:, up_width:] + mlp_bias
     queries = (rotate(pre_qkv[:, :HEAD], cosine, sine).astype(bf16) * HEAD**-0.5).astype(bf16)
     keys_all = rotate(pre_qkv[:, HEAD : 2 * HEAD], cosine, sine).astype(bf16)
     values_all = pre_qkv[:, 2 * HEAD :].astype(bf16)
     attended, totals = attend(queries, keys_all, values_all, starts)
     activated, gelu_back = jax.vjp(gelu_tanh, pre_up)
-    branch = jnp.concatenate([attended, activated.astype(bf16)], axis=1)
+    branch = jnp.concatenate([lanes(attended, 128), activated.astype(bf16)], axis=1)
     branch_sum = sum_scatter(dot_nt(branch, out_all).astype(bf16), "row")
     branch_back, _ = deal_back(branch_sum, None, None)
     output = tokens.astype(f32) + branch_back.astype(f32) + out_bias
@@ -291,7 +860,7 @@
     branch_grad = dot_nn(cotangent_dealt, out_all)
     out_grad = sum_scatter(dot_tn(cotangent_dealt, branch), "col")
     attended_grad = branch_grad[:, :proj_width].astype(bf16)
-    up_pre_grad = gelu_back(branch_grad[:, proj_width:])[0]
+    up_pre_grad = gelu_back(branch_grad[:, 128:])[0]
     query_grad, key_grad, value_grad = attend_back(
         queries, keys_all, values_all, starts, attended, attended_grad, totals
     )
@@ -300,19 +869,15 @@
             rotate(query_grad, cosine, -sine),
             rotate(key_grad, cosine, -sine),
             value_grad,
+            jnp.zeros_like(value_grad),
             up_pre_grad,
         ],
         axis=1,
     ).astype(bf16)
-    in_part = dot_tn(dealt, preact_grad).reshape(cols, feats, in_width)
+    in_part = dot_tn(dealt, preact_grad).astype(bf16).reshape(cols, feats, in_pad)
     bias_part = jnp.sum(preact_grad, axis=0, dtype=f32)
-    bias_rows = jnp.broadcast_to(bias_part[None, None, :], (cols, 8, in_width))
-    in_sum = sum_scatter(
-        jnp.concatenate([in_part, bias_rows], axis=1).reshape(cols * (feats + 8), in_width), "col"
-    )
-    in_grad, in_bias_grad = in_sum[:feats], in_sum[feats]
     normed_grad = sum_scatter(dot_nt(preact_grad, in_all).astype(bf16), "row").astype(f32)
-    scaled = normed_grad * norm_all[0]
+    scaled = normed_grad * gain_all
     mean_first = jnp.mean(scaled, axis=1, keepdims=True)
     mean_second = jnp.mean(scaled * normalized, axis=1, keepdims=True)
     token_grad = inverse_std * (scaled - mean_first - normalized * mean_second)
@@ -341,43 +906,39 @@
         axis=0,
     )
 
-    flip_flags = (False, False, True, True)
-    oriented_grads = (
+    out_grad = jnp.concatenate(
+        [lanes(out_grad[:, :proj_width], up_width), out_grad[:, 128:]], axis=1
+    )
+    old_momentum = jnp.concatenate(
+        [
+            lanes(qkv_momentum, up_width),
+            up_momentum,
+            lanes(proj_momentum.T, up_width),
+            down_momentum.T,
+        ],
+        axis=1,
+    )
+    in_grad, bias_rows, matrix, gram = gram_all(
+        in_part, jnp.broadcast_to(bias_part[None], (8, in_pad)), out_grad, old_momentum, rows, cols
+    )
+    in_bias_grad = bias_rows[0]
+    gradients = (
         in_grad[:, :qkv_width],
-        in_grad[:, qkv_width:],
-        out_grad[:, :proj_width],
-        out_grad[:, proj_width:],
-    )
-    gradients = [g.T if f else g for g, f in zip(oriented_grads, flip_flags)]
+        in_grad[:, up_width:],
+        out_grad[:, :proj_width].T,
+        out_grad[:, up_width:].T,
+    )
     old_states = (qkv_momentum, up_momentum, proj_momentum, down_momentum)
     weights = (qkv_weight, up_weight, proj_weight, down_weight)
     widths = (3 * D, FF, D, FF)
+    sizes = (qkv_width, up_width, proj_width, up_width)
     states = [momentum * old + g for old, g in zip(old_states, gradients)]
-    oriented = []
-    for gradient, state, flipped in zip(gradients, states, flip_flags):
-        direction = gradient + momentum * state
-        direction = direction.T if flipped else direction
-        direction = jnp.pad(direction, ((0, 0), (0, up_width - direction.shape[1])))
-        oriented += [direction, direction]
-    matrix = swap_col(jnp.stack(oriented, axis=0)).reshape(D, up_width)
-    gram = lax.psum(dot_nt(matrix, matrix, precision=high), "row")
-    shrink = 1.0 / (jnp.sqrt(jnp.trace(gram)) + ortho_floor)
-    half = up_width // 2
-    thin = lax.dynamic_slice_in_dim(matrix, (col % 2) * half, half, axis=1) * shrink
-    gram = gram * (shrink * shrink)
-    eye = jnp.eye(D, dtype=f32)
-    for sweep in range(5):
-        squared = dot_nn(gram, gram, precision=high)
-        poly = poly_linear * eye + poly_square * gram + poly_cubic * squared
-        thin = dot_nn(poly, thin, precision=high)
-        if sweep < 4:
-            gram = dot_nn(gram, dot_nn(poly, poly, precision=high), precision=high)
-    returned = swap_col(thin.astype(bf16).reshape(cols, feats, half))
+    returned = swap_col(orthogonalize(gram, matrix).reshape(cols, feats, BLK))
     new_weights = []
     for index in range(4):
         update = jnp.concatenate([returned[2 * index], returned[2 * index + 1]], axis=1)
-        update = update[:, : oriented_grads[index].shape[1]].astype(f32)
-        update = update.T if flip_flags[index] else update
+        update = update[:, : sizes[index]].astype(f32)
+        update = update.T if index >= 2 else update
         new_weights.append(
             weights[index] * (1.0 - rate_matrix * decay_matrix)
             - rate_matrix * 0.2 * math.sqrt(widths[index]) * update
@@ -390,7 +951,7 @@
         qkv_bias, in_bias_grad[:qkv_width], qkv_bias_moment, qkv_bias_square
     )
     mlp_first, mlp_second, mlp_bias_new = adam_step(
-        mlp_bias, in_bias_grad[qkv_width:], mlp_bias_moment, mlp_bias_square
+        mlp_bias, in_bias_grad[up_width:], mlp_bias_moment, mlp_bias_square
     )
     return (
         output,

time: 897 us -> 588 us (0.66)
  waiting for transfers between devices: 534 us -> 125 us
  Pallas kernels: 14.9 us -> 286 us
  matrix products: 141 us -> 32.9 us
  blocking collectives: 37.4 us -> 11.5 us
  local copies, waits for them, and re-layouts: 74.7 us -> 55.6 us
  other arithmetic: 57.9 us -> 43.7 us
    pallas_call x0 -> x3, Pallas kernels: none -> 271 us  [the longest x1 142 us: deal_all(): pl.pallas_call(deal_kernel, out_shape=(shape((group, width), bf16), shape...]
    all_gather x6 -> x2, waiting for transfers between devices: 177 us -> 0.01 us  [gather_row(): return lax.all_gather(x, 'row', axis=0, tiled=True)]
    psum x1 -> x0, waiting for transfers between devices: 137 us -> none  [per_device(): gram = lax.psum(dot_nt(matrix, matrix, precision=high), 'row')]
    dot_general x20 -> x2, matrix products: 117 us -> 11.5 us  [dot_nn(): lax.dot_general(a, b, (((1,), (0,)), ((), ())), preferred_element_type=f3...]
    all_gather x1 -> x0, waiting for transfers between devices: 43.2 us -> none  [per_device(): lax.all_gather(jnp.concatenate([in_weight.astype(bf16), out_weight.astype...]
    unnamed x13 -> x5, waiting for transfers between devices: 26.6 us -> 0.08 us
    all_to_all x3 -> x1, blocking collectives: 37.4 us -> 11.5 us  [swap_col(): return lax.all_to_all(x, 'col', split_axis=0, concat_axis=0, tiled=True)]
    reduce_scatter x3, waiting for transfers between devices: 132 us -> 116 us  [sum_scatter(): return lax.psum_scatter(x, axis, scatter_dimension=0, tiled=True)]
  transfers between devices with their start and end apart: 15 -> 7, of which waited for: 12 -> 5; matrix products, arithmetic and copies ran while one was open for 26% -> 13% of each run, Pallas kernels for 1% -> 24%
where the time goes in v2:
time: 588 us; the launch traced here: 580 us
  Pallas kernels  286 us (49%)
  waiting for transfers between devices  125 us (21%)
  local copies, waits for them, and re-layouts  55.6 us (9%)
  other arithmetic  43.7 us (7%)
  matrix products  32.9 us (6%)
  between operations  15.1 us (3%)
  blocking collectives  11.5 us (2%)
  starting transfers between devices  10.9 us (2%)
    pallas_call x1, Pallas kernels, deal_all(): pl.pallas_call(deal_kernel, out_shape=(shape((group, width), bf16), shape...  142 us
    reduce_scatter x3, waiting for transfers between devices, sum_scatter(): return lax.psum_scatter(x, axis, scatter_dimension=0, tiled=True)  116 us
    pallas_call x1, Pallas kernels, gram_all(): pl.pallas_call(gram_kernel, out_shape=(shape((feats, width), f32), shape(...  67.1 us
    pallas_call x1, Pallas kernels, orthogonalize(): pl.pallas_call(poly_kernel, out_shape=jax.ShapeDtypeStruct((size, width),...  61.4 us
    unnamed x117, local copies, waits for them, and re-layouts  21.1 us
  transfers between devices with their start and end apart: 7, of which 5 were waited for; matrix products, arithmetic and copies ran while one was open for 13% of the time, Pallas kernels for 24%

profile of v2, /device:TPU:0, one launch (start us, length us, event | category | flops | bytes accessed | tf_op | source)
XLA Modules:
  0.0 579.8 jit_solution(6315445096270675222)
XLA Ops:
  14.5 142.2 %deal_all.1 = (bf16[2048,1024]{1,0:T(8,128)(2,1)}, bf16[2048,1024]{1,0:T(8,128)(2,1)}, bf16[1024,896]{1,0:T(8,128)(2,1)S(1)}, f32[8,8,128]{2,1,0:T(8,128)S(1)}, ...) custom-call(bf16[1024,128]{1,0:T(8,128)(2,1)S(1)} %copy-done.3, bf16[1024,128]{1,0:T(8,128)(2,1)S(1)} %copy-done, ...), custom_call_target="tpu_custom_call" | custom-call | tf_op jit(solution)/shard_map/deal_all/pallas_call | solution.py:350
  156.7 7.3 %fusion.36 = f32[2048,512]{0,1:T(8,128)} fusion(bf16[2048,1024]{1,0:T(8,128)(2,1)} %get-tuple-element.38, bf16[1024,896]{1,0:T(8,128)(2,1)S(1)} %get-tuple-element.39), kind=kOutput, calls=%fused_computation.54 | convolution fusion | flops 2147483648 | bytes 9437184 | tf_op jit(solution)/shard_map/dot_general | solution.py:45
  173.6 3.8 multiply_convert_fusion
  177.4 5.2 fusion.31
  183.7 5.6 attend.1
  190.6 6.0 %convolution_convert_fusion = bf16[2048,1024]{1,0:T(8,128)(2,1)} fusion(bf16[2048,64]{0,1:T(8,128)(2,1)S(1)} %copy.229, bf16[2048,256]{0,1:T(8,128)(2,1)} %multiply_convert_fusion, bf16[1024,896]{1,0:T(8,128)(2,1)} %copy-done.12), kind=kOutput, calls=%fused_computation.3 | convolution fusion | flops 1617428480 | bytes 6291456 | tf_op jit(solution)/shard_map/dot_general | solution.py:37
  197.2 4.2 fusion.44
  208.3 9.2 %attend_back.1 = (f32[2048,64]{1,0:T(8,128)S(1)}, f32[2048,64]{1,0:T(8,128)S(1)}, f32[2048,64]{1,0:T(8,128)S(1)}) custom-call(bf16[2048,64]{1,0:T(8,128)(2,1)S(1)} %copy-done.9, bf16[2048,64]{1,0:T(8,128)(2,1)S(1)} %copy-done.11, bf16[2048,64]{1,0:T(8,128)(2,1)S(1)} %copy-done.7, s32[2048,1]{1,0:T(8,128)} %copy-done.2, ...), custom_call_target="tpu_custom_call" | custom-call | flops 1342177280 | bytes 8388608 | tf_op jit(solution)/shard_map/attend_back/pallas_call | solution.py:694
  219.9 6.5 %fusion.22 = (f32[2048,8]{1,0:T(8,128)}, f32[2048,8]{1,0:T(8,128)}, f32[2048,8]{1,0:T(8,128)}, f32[2048,8]{1,0:T(8,128)}, f32[2048,8]{1,0:T(8,128)}, /*index=5*/...) fusion(f32[2048,64]{1,0:T(8,128)S(1)} %get-tuple-element.45, f32[8]{0:T(128)S(1)} %negate_power_fusion, ...), kind=kLoop, calls=%fused_computation.35 | loop fusion | flops 163840 | bytes 794656 | tf_op jit(solution)/shard_map/mul | solution.py:719
  241.2 3.9 fusion.34
  246.4 4.4 convolution_convert_fusion.1
  252.0 5.7 fusion.38
  257.9 26.6 %reduce-scatter.4.cloned.1.call-done = bf16[128,1024]{1,0:T(8,128)(2,1)} async-done(((bf16[2048,1024]{1,0:T(8,128)(2,1)}), bf16[128,1024]{1,0:T(8,128)(2,1)}) %reduce-scatter.4.cloned.1.call-update) | async-done | bytes 262160 | tf_op jit(solution)/shard_map/reduce_scatter | solution.py:747
  285.5 11.5 %all_to_all.15 = bf16[8,128,128]{2,1,0:T(8,128)(2,1)} all-to-all(bf16[8,128,128]{2,1,0:T(8,128)(2,1)S(1)} %bitcast_bitcast_fusion.1), channel_id=1, replica_groups=mesh['row'=16,'col'=8] {'col'}, dimensions={0} | all-to-all | bytes 524288 | tf_op jit(solution)/shard_map/all_to_all | solution.py:743
  300.6 67.9 %reduce-scatter.6.cloned.1.call-done = bf16[128,1024]{1,0:T(8,128)(2,1)} async-done(((bf16[2048,1024]{1,0:T(8,128)(2,1)}), bf16[128,1024]{1,0:T(8,128)(2,1)}) %reduce-scatter.6.cloned.1.call-update) | async-done | bytes 262160 | tf_op jit(solution)/shard_map/reduce_scatter | solution.py:747
  371.6 4.3 all-to-all-start.1
  376.5 7.8 %all-to-all-done.1 = bf16[8,144,128]{2,1,0:T(8,128)(2,1)S(1)} async-done(((bf16[8,144,128]{2,1,0:T(8,128)(2,1)}), bf16[8,144,128]{2,1,0:T(8,128)(2,1)S(1)}, u32[]{:S(2)}, u32[]{:S(2)}) %all-to-all-start.1) | async-done | bytes 294944 | tf_op jit(solution)/shard_map/all_to_all | solution.py:743
  385.1 5.3 convolution_convert_fusion.2
  390.4 21.0 %reduce-scatter.8.cloned.1.call-done = f32[128,384]{1,0:T(8,128)} async-done(((f32[1024,384]{1,0:T(8,128)}), f32[128,384]{1,0:T(8,128)}) %reduce-scatter.8.cloned.1.call-update) | async-done | bytes 196624 | tf_op jit(solution)/shard_map/reduce_scatter | solution.py:747
  412.5 67.1 %gram_all.1 = (f32[128,512]{1,0:T(8,128)S(1)}, f32[8,512]{1,0:T(8,128)S(1)}, f32[8,128,128]{2,1,0:T(8,128)S(1)}, f32[4608,128]{1,0:T(8,128)S(1)}) custom-call(bf16[8,128,512]{2,1,0:T(8,128)(2,1)S(1)} %bitcast.81, f32[8,512]{1,0:T(8,128)S(1)} %broadcast_in_dim.79.bias_ref, f32[128,512]{1,0:T(8,128)S(1)} %pad_maximum_fusion.1.out_grad_ref, ...), custom_call_target="tpu_custom_call" | custom-call | tf_op jit(solution)/shard_map/gram_all/pallas_call | solution.py:646
  479.6 61.4 %orthogonalize.1 = bf16[1024,128]{1,0:T(8,128)(2,1)S(1)} custom-call(f32[4608,128]{1,0:T(8,128)S(1)} %get-tuple-element.50.gram_ref, f32[8,128,128]{2,1,0:T(8,128)S(1)} %get-tuple-element.51.matrix_ref), custom_call_target="tpu_custom_call" | custom-call | flops 51539607552 | bytes 12582912 | tf_op jit(solution)/shard_map/orthogonalize/pallas_call | solution.py:626
  541.9 5.6 all-to-all-start.2
  557.8 5.6 gather_fusion
  565.6 5.8 %gather_fusion.1 = bf16[1024,128]{1,0:T(8,128)(2,1)S(1)} fusion(bf16[18432,128]{1,0:T(8,128)(2,1)} %all-gather.5.cloned.1.call-done, s32[1024]{0:T(1024)S(1)} %broadcast_clamp_fusion), kind=kCustom, calls=%fused_computation.1 | custom fusion | bytes 528384 | tf_op jit(solution)/shard_map/gather | solution.py:751
  (223 shorter events, 70.7 us)
Async XLA Ops:
  7.2 277.3 %reduce-scatter.4.cloned.1.call-start = ((), (), s32[]{:S(2)}) async-start(), calls=%async_computation.6 | async-start | bytes 4456448 | tf_op jit(solution)/shard_map/reduce_scatter | solution.py:747
  170.1 13.6 %copy-start.6 = (bf16[2048,64]{1,0:T(8,128)(2,1)}, bf16[2048,64]{1,0:T(8,128)(2,1)S(1)}, u32[]{:S(2)}) copy-start(bf16[2048,64]{1,0:T(8,128)(2,1)S(1)} %slice.213.v_ref) | copy-start | bytes 786436
  173.6 10.1 %copy-start.2 = (s32[2048,1]{1,0:T(8,128)}, s32[2048,1]{1,0:T(8,128)S(1)}, u32[]{:S(2)}) copy-start(s32[2048,1]{1,0:T(8,128)S(1)} %copy.196.start_ref) | copy-start | bytes 24580
  196.7 171.8 %reduce-scatter.6.cloned.1.call-start = ((), (), s32[]{:S(2)}) async-start(), calls=%async_computation.8 | async-start | bytes 4456448 | tf_op jit(solution)/shard_map/reduce_scatter | solution.py:747
  250.8 160.7 %reduce-scatter.8.cloned.1.call-start = ((), (), s32[]{:S(2)}) async-start(), calls=%async_computation.10 | async-start | bytes 1769472 | tf_op jit(solution)/shard_map/reduce_scatter | solution.py:747
  257.8 39.3 %copy-start.35 = (s32[16384]{0:T(1024)S(1)}, s32[16384]{0:T(1024)}, u32[]{:S(2)}) copy-start(s32[16384]{0:T(1024)} %param.24) | copy-start | bytes 196612
  257.8 39.8 %copy-start.37 = (f32[64,128]{1,0:T(8,128)S(1)}, f32[64,128]{1,0:T(8,128)}, u32[]{:S(2)}) copy-start(f32[64,128]{1,0:T(8,128)} %param.34) | copy-start | bytes 98308
  257.8 39.9 %copy-start.36 = (f32[128,192]{0,1:T(8,128)S(1)}, f32[128,192]{0,1:T(8,128)}, u32[]{:S(2)}) copy-start(f32[128,192]{0,1:T(8,128)} %param.32) | copy-start | bytes 294916
  257.8 40.0 %copy-start.33 = (f32[256,128]{1,0:T(8,128)S(1)}, f32[256,128]{1,0:T(8,128)}, u32[]{:S(2)}) copy-start(f32[256,128]{1,0:T(8,128)} %param.35) | copy-start | bytes 393220
  257.8 40.4 %copy-start.1 = (bf16[1024,128]{1,0:T(8,128)(2,1)S(1)}, bf16[1024,128]{1,0:T(8,128)(2,1)}, u32[]{:S(2)}) copy-start(bf16[1024,128]{1,0:T(8,128)(2,1)} %cotangent_ref.1) | copy-start | bytes 786436
  257.8 40.5 %copy-start.28 = (f32[128,256]{1,0:T(8,128)S(1)}, f32[128,256]{1,0:T(8,128)}, u32[]{:S(2)}) copy-start(f32[128,256]{1,0:T(8,128)} %param.33) | copy-start | bytes 393220
  257.8 300.0 %all-gather.3.cloned.1.call-start = ((), (), s32[]{:S(2)}) async-start(), calls=%async_computation.7 | async-start | bytes 4456448 | tf_op jit(solution)/shard_map/all_gather | solution.py:739
  300.4 76.0 %copy-start.27 = (f32[128,256]{1,0:T(8,128)S(1)}, f32[128,256]{1,0:T(8,128)}, u32[]{:S(2)}) copy-start(f32[128,256]{1,0:T(8,128)} %param.26) | copy-start | bytes 393220
  371.6 12.7 %all-to-all-start.1 = ((bf16[8,144,128]{2,1,0:T(8,128)(2,1)}), bf16[8,144,128]{2,1,0:T(8,128)(2,1)S(1)}, u32[]{:S(2)}, u32[]{:S(2)}) async-start(bf16[8,144,128]{2,1,0:T(8,128)(2,1)} %fusion.58), calls=%async_computation.3 | async-start | bytes 589824 | tf_op jit(solution)/shard_map/all_to_all | solution.py:743
  375.9 188.4 %all-gather.5.cloned.1.call-start = ((), (), s32[]{:S(2)}) async-start(), calls=%async_computation.9 | async-start | bytes 5013504 | tf_op jit(solution)/shard_map/all_gather | solution.py:739
  385.1 26.4 %copy-start.48 = (pred[256]{0:T(512)(128)(4,1)S(1)}, pred[256]{0:T(512)(128)(4,1)}, u32[]{:S(2)}) copy-start(pred[256]{0:T(512)(128)(4,1)} %constant.163.clone.1) | copy-start | bytes 772
  479.6 68.0 %copy-start.24 = (f32[128,384]{1,0:T(8,128)S(1)}, f32[128,384]{1,0:T(8,128)}, u32[]{:S(2)}) copy-start(f32[128,384]{1,0:T(8,128)} %reduce-scatter.8.cloned.1.call-done) | copy-start | bytes 589828
  541.1 12.3 %copy-start.46 = (f32[192]{0:T(256)S(1)}, f32[192]{0:T(256)}, u32[]{:S(2)}) copy-start(f32[192]{0:T(256)} %param.39) | copy-start | bytes 2308
  541.1 12.3 %copy-start.47 = (f32[192]{0:T(256)S(1)}, f32[192]{0:T(256)}, u32[]{:S(2)}) copy-start(f32[192]{0:T(256)} %param.38) | copy-start | bytes 2308
  541.9 13.1 %all-to-all-start.2 = ((bf16[8,128,128]{1,2,0:T(8,128)(2,1)}), bf16[8,128,128]{1,2,0:T(8,128)(2,1)S(1)}, u32[]{:S(2)}, u32[]{:S(2)}) async-start(bf16[8,128,128]{1,2,0:T(8,128)(2,1)} %copy.219), calls=%async_computation.5 | async-start | bytes 524288 | tf_op jit(solution)/shard_map/all_to_all | solution.py:743
  547.5 8.4 %copy-start.34 = (f32[64,128]{1,0:T(8,128)S(1)}, f32[64,128]{1,0:T(8,128)}, u32[]{:S(2)}) copy-start(f32[64,128]{1,0:T(8,128)} %param.27) | copy-start | bytes 98308
  547.5 9.0 %copy-start.30 = (f32[128,192]{0,1:T(8,128)S(1)}, f32[128,192]{0,1:T(8,128)}, u32[]{:S(2)}) copy-start(f32[128,192]{0,1:T(8,128)} %param.25) | copy-start | bytes 294916
  547.5 9.6 %copy-start.29 = (f32[256,128]{1,0:T(8,128)S(1)}, f32[256,128]{1,0:T(8,128)}, u32[]{:S(2)}) copy-start(f32[256,128]{1,0:T(8,128)} %param.28) | copy-start | bytes 393220
  553.3 10.1 %copy-start.4 = (bf16[1024,128]{1,0:T(8,128)(2,1)S(1)}, bf16[1024,128]{1,0:T(8,128)(2,1)}, u32[]{:S(2)}) copy-start(bf16[1024,128]{1,0:T(8,128)(2,1)} %tokens_ref.1) | copy-start | bytes 786436
  (32 other events, 129.1 us)
Sparse Core Ops, SparseCore 0:
  196.8 87.6 reduce-scatter.3
  289.0 79.3 reduce-scatter.5
  370.9 40.5 reduce-scatter.7
  413.8 77.6 all-gather.2
  494.4 58.8 all-gather.4

commit v3 on v2

--- a/solution.py
+++ b/solution.py
@@ -52,8 +52,66 @@
     return (key_at >= start_ref[pl.ds(first, BLOCK), :]) & (key_at <= query_at)
 
 
-def attend_kernel(q_ref, k_ref, v_ref, start_ref, out_ref, total_ref):
-    for first in range(0, q_ref.shape[0], BLOCK):
+def turning(table_ref, rows):
+    lane = lax.broadcasted_iota(jnp.int32, (32, 2 * HEAD), 1) % HEAD
+    entry = lax.broadcasted_iota(jnp.int32, (32, 2 * HEAD), 0) % 16
+    half_rot = ROT // 2
+
+    def spread(where, value):
+        picks = jnp.where(where, value, 0.0).astype(bf16)
+        return dot_tn(table_ref[:, rows], picks)
+
+    cosine = spread((lane < ROT) & (entry == lane % half_rot), 1.0)
+    cosine = cosine + jnp.where(lane[:1] < ROT, 0.0, 1.0)
+    lower = spread((lane < half_rot) & (entry == lane + half_rot), -1.0)
+    upper = spread((lane >= half_rot) & (lane < ROT) & (entry == lane), 1.0)
+    return cosine, lower, upper
+
+
+def turned(values, tables, back):
+    cosine, lower, upper = tables
+    half_rot = ROT // 2
+    moved = (
+        pltpu.roll(values, 2 * HEAD - half_rot, 1) * lower + pltpu.roll(values, half_rot, 1) * upper
+    )
+    return values * cosine - moved if back else values * cosine + moved
+
+
+def forward_kernel(
+    dealt_ref,
+    cotangent_ref,
+    weight_ref,
+    bias_ref,
+    table_ref,
+    start_ref,
+    q_ref,
+    k_ref,
+    v_ref,
+    slope_ref,
+    branch_ref,
+    total_ref,
+    partial_ref,
+    out_part_ref,
+):
+    width = bias_ref.shape[1]
+    in_weight, out_weight = weight_ref[:, :width], weight_ref[:, width:]
+    inner = math.sqrt(2.0 / math.pi)
+    firsts = range(0, dealt_ref.shape[0], BLOCK)
+    for first in firsts:
+        rows = pl.ds(first, BLOCK)
+        pre = dot_nn(dealt_ref[rows, :], in_weight) + bias_ref[...]
+        pair = turned(pre[:, : 2 * HEAD], turning(table_ref, rows), False).astype(bf16)
+        q_ref[rows, :] = (pair[:, :HEAD] * HEAD**-0.5).astype(bf16)
+        k_ref[rows, :] = pair[:, HEAD:]
+        v_ref[rows, :] = pre[:, 2 * HEAD : 3 * HEAD].astype(bf16)
+        up = pre[:, 4 * HEAD :]
+        square = up * up
+        bent = jnp.tanh(inner * (up + 0.044715 * square * up))
+        branch_ref[rows, 2 * HEAD :] = (0.5 * up * (1.0 + bent)).astype(bf16)
+        slope_ref[rows, :] = 0.5 * (1.0 + bent) + 0.5 * up * (1.0 - bent * bent) * (
+            inner * (1.0 + 3.0 * 0.044715 * square)
+        )
+    for first in firsts:
         rows, keys = pl.ds(first, BLOCK), first + BLOCK
         scores = dot_nt(q_ref[rows, :], k_ref[:keys, :])
         scores = jnp.where(allowed_keys(start_ref, first, keys), scores, masked_score)
@@ -61,27 +119,184 @@
         raw = jnp.exp(scores - top)
         total = jnp.sum(raw, axis=1, keepdims=True)
         attended = dot_nn(raw.astype(bf16), v_ref[:keys, :]) / total
-        out_ref[rows, :] = attended.astype(bf16)
+        branch_ref[rows, : 2 * HEAD] = jnp.concatenate(
+            [attended, jnp.zeros_like(attended)], axis=1
+        ).astype(bf16)
         total_ref[rows, :] = top + jnp.log(total)
-
-
-def attend_back_kernel(
-    q_ref, k_ref, v_ref, start_ref, out_ref, grad_ref, total_ref, dq_ref, dk_ref, dv_ref
+        partial_ref[rows, :] = dot_nt(branch_ref[rows, :], out_weight).astype(bf16)
+    for first in range(0, cotangent_ref.shape[1], BLOCK):
+        lanes = slice(first, first + BLOCK)
+        out_part_ref[lanes, :] = dot_tn(cotangent_ref[:, lanes], branch_ref[...])
+
+
+def backward_kernel(
+    dealt_ref,
+    cotangent_ref,
+    weight_ref,
+    table_ref,
+    start_ref,
+    q_ref,
+    k_ref,
+    v_ref,
+    slope_ref,
+    branch_ref,
+    total_ref,
+    branch_part_ref,
+    out_part_ref,
+    in_part_ref,
+    bias_part_ref,
+    normed_part_ref,
+    branch_sum_ref,
+    out_grad_ref,
+    grad_ref,
+    pre_ref,
+    dk_ref,
+    dv_ref,
+    out_parts,
+    pairs,
+    slots,
+    *sems,
 ):
+    at = Place()
+    branch_rows = RowSum(at, branch_part_ref, pairs, slots, sems[:4])
+    swap_out = ColSwap(at, lambda c: out_part_ref.at[c], lambda c: out_parts.at[c], sems[4:])
+    meet(row_peers(at) + col_peers(at))
+    branch_rows.start()
+    swap_out.start()
+    out_parts[at.col] = out_part_ref[at.col]
+    width = pre_ref.shape[1]
+    in_weight, out_weight = weight_ref[:, :width], weight_ref[:, width:]
+    firsts = range(0, dealt_ref.shape[0], BLOCK)
+    for first in firsts:
+        rows = pl.ds(first, BLOCK)
+        branch_grad = dot_nn(cotangent_ref[rows, :], out_weight)
+        grad_ref[rows, :] = branch_grad[:, :HEAD].astype(bf16)
+        pre_ref[rows, 4 * HEAD :] = (branch_grad[:, 2 * HEAD :] * slope_ref[rows, :]).astype(bf16)
     dk_ref[...] = jnp.zeros_like(dk_ref)
     dv_ref[...] = jnp.zeros_like(dv_ref)
-    for first in range(0, q_ref.shape[0], BLOCK):
+    branch_rows.middle()
+    for first in reversed(firsts):
         rows, keys = pl.ds(first, BLOCK), first + BLOCK
         query, grad = q_ref[rows, :], grad_ref[rows, :]
         key, value = k_ref[:keys, :], v_ref[:keys, :]
         scores = dot_nt(query, key)
         allowed = allowed_keys(start_ref, first, keys)
         prob = jnp.where(allowed, jnp.exp(scores - total_ref[rows, :]), 0.0)
-        delta = jnp.sum(grad.astype(f32) * out_ref[rows, :].astype(f32), axis=1, keepdims=True)
+        delta = jnp.sum(
+            grad.astype(f32) * branch_ref[rows, :HEAD].astype(f32), axis=1, keepdims=True
+        )
         score_grad = (prob * (dot_nt(grad, value) - delta)).astype(bf16)
-        dq_ref[rows, :] = dot_nn(score_grad, key) * HEAD**-0.5
         dk_ref[:keys, :] += dot_tn(score_grad, query)
         dv_ref[:keys, :] += dot_tn(prob.astype(bf16), grad)
+        pair = jnp.concatenate([dot_nn(score_grad, key) * HEAD**-0.5, dk_ref[rows, :]], axis=1)
+        pre_ref[rows, : 2 * HEAD] = turned(pair, turning(table_ref, rows), True).astype(bf16)
+        dv = dv_ref[rows, :]
+        pre_ref[rows, 2 * HEAD : 4 * HEAD] = jnp.concatenate(
+            [dv, jnp.zeros_like(dv)], axis=1
+        ).astype(bf16)
+        normed_part_ref[rows, :] = dot_nt(pre_ref[rows, :], in_weight).astype(bf16)
+    feats = in_part_ref.shape[1]
+    each = BLOCK // feats
+    for first in range(0, dealt_ref.shape[1], BLOCK):
+        part = dot_tn(dealt_ref[:, first : first + BLOCK], pre_ref[...])
+        for index in range(each):
+            in_part_ref[first // feats + index] = part[
+                index * feats : (index + 1) * feats, :
+            ].astype(bf16)
+    bias = jnp.sum(pre_ref[...].astype(f32), axis=0, keepdims=True)
+    bias_part_ref[...] = jnp.broadcast_to(bias, bias_part_ref.shape)
+    swap_out.arrived()
+    total = sum(out_parts[c] for c in range(at.cols))
+    filled = jnp.zeros((total.shape[0], width // 2 - 2 * HEAD), f32)
+    out_grad_ref[:, : 2 * HEAD] = total[:, : 2 * HEAD]
+    out_grad_ref[:, 2 * HEAD : width // 2] = filled
+    out_grad_ref[:, width // 2 :] = total[:, 2 * HEAD :]
+    branch_sum_ref[...] = branch_rows.finish().astype(bf16)
+    branch_rows.sent()
+    swap_out.sent()
+
+
+def local_call(kernel, out_shape, scratch, flops, name):
+    return pl.pallas_call(
+        kernel,
+        out_shape=out_shape,
+        scratch_shapes=scratch,
+        compiler_params=pltpu.CompilerParams(vmem_limit_bytes=VMEM_LIMIT),
+        cost_estimate=pl.CostEstimate(flops=flops, bytes_accessed=1 << 24, transcendentals=0),
+        name=name,
+    )
+
+
+def forward(dealt, cotangent, weight, bias, table, starts):
+    rows, width = dealt.shape
+    up = bias.shape[1] - 4 * HEAD
+    branch = up + 2 * HEAD
+    shape = jax.ShapeDtypeStruct
+    head = shape((rows, HEAD), bf16)
+    return local_call(
+        forward_kernel,
+        (
+            *(head, head, head),
+            shape((rows, up), f32),
+            shape((rows, branch), bf16),
+            shape((rows, 1), f32),
+            shape((rows, width), bf16),
+            shape((width, branch), f32),
+        ),
+        [],
+        25 * 10**9,
+        "forward",
+    )(dealt, cotangent, weight, bias, table, starts)
+
+
+def remote_call(kernel, identity, out_shape, in_specs, scratch, flops, name):
+    return pl.pallas_call(
+        kernel,
+        out_shape=out_shape,
+        in_specs=in_specs,
+        out_specs=(VMEM_SPEC,) * len(out_shape),
+        scratch_shapes=scratch,
+        compiler_params=pltpu.CompilerParams(
+            collective_id=identity, has_side_effects=True, vmem_limit_bytes=VMEM_LIMIT
+        ),
+        cost_estimate=pl.CostEstimate(flops=flops, bytes_accessed=1 << 24, transcendentals=0),
+        name=name,
+    )
+
+
+def backward(dealt, cotangent, weight, table, starts, kept, branch_part, out_part, rows, cols):
+    tokens, width = dealt.shape
+    in_width = 4 * HEAD + kept[3].shape[1]
+    out_width = out_part.shape[1]
+    feats, piece, chips = width // cols, tokens // rows, rows // 2
+    shape = jax.ShapeDtypeStruct
+    return remote_call(
+        backward_kernel,
+        2,
+        (
+            shape((cols, feats, in_width), bf16),
+            shape((8, in_width), f32),
+            shape((tokens, width), bf16),
+            shape((piece, width), bf16),
+            shape((feats, in_width), f32),
+        ),
+        [VMEM_SPEC] * 13,
+        [
+            pltpu.VMEM((tokens, HEAD), bf16),
+            pltpu.VMEM((tokens, in_width), bf16),
+            pltpu.VMEM((tokens, HEAD), f32),
+            pltpu.VMEM((tokens, HEAD), f32),
+            pltpu.VMEM((cols, feats, out_width), f32),
+            *sum_scratch(piece, width, chips),
+            *swap_sems(cols),
+        ],
+        30 * 10**9,
+        "backward",
+    )(
+        *(dealt, cotangent, weight, table, starts, *kept),
+        branch_part.reshape(chips, 2, piece, width),
+        out_part.reshape(cols, feats, out_width),
+    )
 
 
 VMEM_LIMIT = 48 * 1024 * 1024
@@ -105,6 +320,8 @@
         self.chips = self.rows // 2
         self.chip, self.core = self.row // 2, self.row % 2
         self.twin = (self.chip * 2 + 1 - self.core, self.col)
+        self.ring = self.chips // 2
+        self.y, self.z = self.chip // self.ring, self.chip % self.ring
 
     def chip_at(self, step):
         return lax.rem(self.chip + step, self.chips)
@@ -124,63 +341,120 @@
 
 
 class RowGather:
+    OWN, PARTNER, BELOW, ABOVE, BELOW_PARTNER, ABOVE_PARTNER, FAR, FAR_PARTNER = range(8)
+
     def __init__(self, at, slot, sems):
         self.at, self.slot = at, slot
-        self.send, self.recv, self.pass_send, self.pass_recv = sems
-
-    def outgoing(self, step, src):
-        at = self.at
+        self.sems = sems
+        ring, z, y = at.ring, at.z, at.y
+        self.chips = [
+            y * ring + z,
+            (1 - y) * ring + z,
+            y * ring + lax.rem(z + ring - 1, ring),
+            y * ring + lax.rem(z + 1, ring),
+            (1 - y) * ring + lax.rem(z + ring - 1, ring),
+            (1 - y) * ring + lax.rem(z + 1, ring),
+            y * ring + lax.rem(z + 2, ring),
+            (1 - y) * ring + lax.rem(z + 2, ring),
+        ]
+
+    def row_of(self, which):
+        return self.chips[which] * 2 + self.at.core
+
+    def block(self, which):
+        return self.slot(self.row_of(which))
+
+    def part(self, which, upper):
+        ref = self.block(which)
+        half = ref.shape[0] // 2
+        return ref.at[pl.ds(0 if upper else half, half), :]
+
+    def hop(self, tag, src, dst, to):
+        send, recv = self.sems[0], self.sems[1]
+        return remote(src, dst, send.at[tag], recv.at[tag], (self.row_of(to), self.at.col))
+
+    def took(self, tag, ref):
+        self.hop(tag, ref, ref, self.PARTNER).wait_recv()
+
+    def passing(self, which, src=None):
+        send, recv = self.sems[2], self.sems[3]
+        ref = self.block(which)
         return remote(
-            src,
-            self.slot(at.row),
-            self.send.at[step],
-            self.recv.at[step],
-            (at.chip_row(step), at.col),
+            ref if src is None else src, ref, send.at[which], recv.at[which], self.at.twin
         )
 
-    def passing(self, step, src, row):
-        return remote(
-            src, self.slot(row), self.pass_send.at[step], self.pass_recv.at[step], self.at.twin
-        )
-
-    def came_from(self, step):
-        return self.at.chip_row(self.at.chips - step)
+    def hops(self):
+        own, src = self.block(self.OWN), self.src
+        partner = self.block(self.PARTNER)
+        below, above = self.part(self.BELOW, True), self.part(self.ABOVE, False)
+        far_below = self.part(self.BELOW_PARTNER, True)
+        far_above = self.part(self.ABOVE_PARTNER, False)
+        return {
+            "start": [
+                (0, src, own, self.PARTNER),
+                (1, src, own, self.ABOVE),
+                (2, src, own, self.BELOW),
+            ],
+            "partner": [(3, partner, partner, self.ABOVE), (4, partner, partner, self.BELOW)],
+            "below": [(5, below, below, self.ABOVE)],
+            "above": [(6, above, above, self.BELOW)],
+            "far_below": [(7, far_below, far_below, self.ABOVE)],
+            "far_above": [(8, far_above, far_above, self.BELOW)],
+        }
+
+    def go(self, stage):
+        for hop in self.hops()[stage]:
+            self.hop(*hop).start()
 
     def start(self, src):
         self.src = src
-        for step in range(1, self.at.chips):
-            self.outgoing(step, src).start()
-        self.passing(0, src, self.at.row).start()
+        self.go("start")
+        self.passing(self.OWN, src).start()
+
+    def landed(self, which, then):
+        self.passing(which).start()
+        if then is not None:
+            then(self.row_of(which))
 
     def forward(self, then=None):
-        for step in range(1, self.at.chips):
-            row = self.came_from(step)
+        self.took(1, self.block(self.BELOW))
+        self.go("below")
+        self.took(2, self.block(self.ABOVE))
+        self.go("above")
+        self.landed(self.BELOW, then)
+        self.landed(self.ABOVE, then)
+        self.took(0, self.block(self.PARTNER))
+        self.go("partner")
+        self.landed(self.PARTNER, then)
+        self.took(3, self.block(self.BELOW_PARTNER))
+        self.go("far_below")
+        self.took(4, self.block(self.ABOVE_PARTNER))
+        self.go("far_above")
+        self.landed(self.BELOW_PARTNER, then)
+        self.landed(self.ABOVE_PARTNER, then)
+        self.took(5, self.part(self.FAR, True))
+        self.took(6, self.part(self.FAR, False))
+        self.landed(self.FAR, then)
+        self.took(7, self.part(self.FAR_PARTNER, True))
+        self.took(8, self.part(self.FAR_PARTNER, False))
+        self.landed(self.FAR_PARTNER, then)
+
+    def finish(self, then=None):
+        send, recv = self.sems[2], self.sems[3]
+        for which in range(8):
+            row = self.chips[which] * 2 + 1 - self.at.core
             slot = self.slot(row)
-            remote(
-                slot, slot, self.send.at[step], self.recv.at[step], (row, self.at.col)
-            ).wait_recv()
-            self.passing(step, slot, row).start()
+            remote(slot, slot, send.at[which], recv.at[which], self.at.twin).wait_recv()
             if then is not None:
                 then(row)
 
-    def finish(self, then=None):
-        at = self.at
-        for step in range(at.chips):
-            row = at.chip_at(at.chips - step) * 2 + 1 - at.core
-            slot = self.slot(row)
-            remote(
-                slot, slot, self.pass_send.at[step], self.pass_recv.at[step], at.twin
-            ).wait_recv()
-            if then is not None:
-                then(row)
-
     def sent(self):
-        for step in range(1, self.at.chips):
-            self.outgoing(step, self.src).wait_send()
-        self.passing(0, self.src, self.at.row).wait_send()
-        for step in range(1, self.at.chips):
-            row = self.came_from(step)
-            self.passing(step, self.slot(row), row).wait_send()
+        for stage in self.hops().values():
+            for hop in stage:
+                self.hop(*hop).wait_send()
+        self.passing(self.OWN, self.src).wait_send()
+        for which in range(1, 8):
+            self.passing(which).wait_send()
 
 
 class ColSwap:
@@ -211,8 +485,132 @@
             self.outgoing(step).wait_send()
 
 
-def gather_sems(chips):
-    return [pltpu.SemaphoreType.DMA((chips,))] * 4
+class RowSum:
+    SEMS = 4
+
+    def __init__(self, at, part, pairs, slots, sems):
+        self.at, self.part, self.pairs, self.slots = at, part, pairs, slots
+        self.twin_send, self.twin_recv, self.send, self.recv = sems
+
+    def to_twin(self):
+        at = self.at
+        return remote(
+            self.part.at[:, 1 - at.core],
+            self.pairs,
+            self.twin_send.at[0],
+            self.twin_recv.at[0],
+            at.twin,
+        )
+
+    def outgoing(self, step):
+        at = self.at
+        return remote(
+            self.pairs.at[at.chip_at(step)],
+            self.slots.at[at.chip],
+            self.send.at[step],
+            self.recv.at[step],
+            (at.chip_row(step), at.col),
+        )
+
+    def start(self):
+        self.to_twin().start()
+
+    def middle(self):
+        at = self.at
+        self.to_twin().wait_recv()
+
+        for step in (4, 1, 2, 3, 5, 6, 7, 0):
+            chip = at.chip_at(step)
+            both = self.part[chip, at.core].astype(f32) + self.pairs[chip].astype(f32)
+            self.pairs[chip] = both.astype(bf16)
+            if step > 0:
+                self.outgoing(step).start()
+
+    def finish(self):
+        at = self.at
+        total = self.pairs[at.chip].astype(f32)
+        for step in range(1, at.chips):
+            chip = at.chip_at(at.chips - step)
+            slot = self.slots.at[chip]
+            remote(
+                slot, slot, self.send.at[step], self.recv.at[step], (chip * 2 + at.core, at.col)
+            ).wait_recv()
+            total = total + self.slots[chip].astype(f32)
+        return total
+
+    def sent(self):
+        self.to_twin().wait_send()
+        for step in range(1, self.at.chips):
+            self.outgoing(step).wait_send()
+
+
+def sum_scratch(piece, width, chips):
+    dma = pltpu.SemaphoreType.DMA
+    return [
+        pltpu.VMEM((chips, piece, width), bf16),
+        pltpu.VMEM((chips, piece, width), bf16),
+        dma((1,)),
+        dma((1,)),
+        dma((chips,)),
+        dma((chips,)),
+    ]
+
+
+class RowSpread:
+    def __init__(self, at, whole, sems):
+        self.at, self.whole = at, whole
+        self.send, self.recv, self.pass_send, self.pass_recv = sems
+
+    def outgoing(self, step):
+        at = self.at
+        slot = self.whole.at[at.row]
+        return remote(
+            slot, slot, self.send.at[step], self.recv.at[step], (at.chip_row(step), at.col)
+        )
+
+    def passing(self, step):
+        at = self.at
+        slot = self.whole.at[at.chip_row(at.chips - step)]
+        return remote(slot, slot, self.pass_send.at[step], self.pass_recv.at[step], at.twin)
+
+    def start(self):
+        for step in (4, 1, 2, 3, 5, 6, 7):
+            self.outgoing(step).start()
+        self.passing(0).start()
+
+    def middle(self):
+        at = self.at
+        for step in (4, 1, 2, 3, 5, 6, 7):
+            row = at.chip_row(at.chips - step)
+            slot = self.whole.at[row]
+            remote(slot, slot, self.send.at[step], self.recv.at[step], (row, at.col)).wait_recv()
+            self.passing(step).start()
+
+    def finish(self):
+        at = self.at
+        for step in range(at.chips):
+            slot = self.whole.at[at.chip_at(at.chips - step) * 2 + 1 - at.core]
+            remote(
+                slot, slot, self.pass_send.at[step], self.pass_recv.at[step], at.twin
+            ).wait_recv()
+
+    def sent(self):
+        for step in range(1, self.at.chips):
+            self.outgoing(step).wait_send()
+        for step in range(self.at.chips):
+            self.passing(step).wait_send()
+
+
+def row_peers(at):
+    return [(at.chip_row(step), at.col) for step in range(1, at.chips)] + [at.twin]
+
+
+def col_peers(at):
+    return [(at.row, at.col_at(step)) for step in range(1, at.cols)]
+
+
+def gather_sems():
+    return [pltpu.SemaphoreType.DMA((count,)) for count in (9, 9, 8, 8)]
 
 
 def swap_sems(cols):
@@ -266,7 +664,7 @@
     swap_vector = ColSwap(at, lambda c: vector_ref, lambda c: vector_all_ref.at[c], some(2))
 
     meet(
-        [(at.chip_row(step), at.col) for step in range(1, at.chips)]
+        [(first_tokens.row_of(which), at.col) for which in (1, 2, 3)]
         + [at.twin]
         + [(at.row, at.col_at(step)) for step in range(1, at.cols)]
     )
@@ -345,7 +743,6 @@
     group = total // cols
     piece = group // rows
     width = feats * cols
-    chips = rows // 2
     shape = jax.ShapeDtypeStruct
     return pl.pallas_call(
         deal_kernel,
@@ -365,12 +762,15 @@
             pltpu.VMEM((total, feats), f32),
             pltpu.VMEM((cols * piece, feats), f32),
             *([pltpu.VMEM((cols, piece, feats), bf16)] * 4),
-            *(gather_sems(chips) * 4),
+            *(gather_sems() * 4),
             *(swap_sems(cols) * 4),
         ],
         compiler_params=pltpu.CompilerParams(
             collective_id=0, has_side_effects=True, vmem_limit_bytes=VMEM_LIMIT
         ),
+        cost_estimate=pl.CostEstimate(
+            flops=100 * 10**9, bytes_accessed=1 << 24, transcendentals=0
+        ),
         name="deal_all",
     )(tokens, cotangent, pick, weight, vectors)
 
@@ -392,10 +792,12 @@
     bias_ref,
     out_grad_ref,
     momentum_ref,
+    normed_part_ref,
     in_grad_ref,
     bias_grad_ref,
     matrix_ref,
     gram_ref,
+    normed_sum_ref,
     parts,
     biases,
     chunks,
@@ -403,10 +805,13 @@
     from_twin,
     half_sum,
     slices,
+    pairs,
+    slots,
     *sems,
 ):
     at = Place()
-    sems = list(sems)
+    normed_rows = RowSum(at, normed_part_ref, pairs, slots, sems[:4])
+    sems = list(sems[4:])
 
     def some(count):
         taken, sems[:count] = sems[:count], []
@@ -425,8 +830,9 @@
         return other, ((other // 2) * 2 + at.core, first_col + other % 2)
 
     peers = [member(step)[1] for step in range(1, count)]
-    meet([(at.row, at.col_at(step)) for step in range(1, at.cols)] + [at.twin] + peers)
+    meet(row_peers(at) + col_peers(at) + peers)
     swap_part.start()
+    normed_rows.start()
     swap_bias.start()
     parts[at.col] = in_part_ref[at.col]
     biases[at.col] = bias_ref[...]
@@ -443,6 +849,7 @@
         state = momentum * momentum_ref[:, lanes] + grad
         chunks[index] = grad + momentum * state
     swap_chunk.start()
+    normed_rows.middle()
     matrix_ref[at.col] = chunks[at.col]
     swap_bias.arrived()
     bias_grad_ref[...] = sum(biases[c] for c in range(at.cols))
@@ -522,6 +929,8 @@
     for step in range(1, count):
         give(step).wait_send()
         spread(step).wait_send()
+    normed_sum_ref[...] = normed_rows.finish()
+    normed_rows.sent()
     for moved in (swap_part, swap_bias, swap_chunk):
         moved.sent()
 
@@ -529,7 +938,92 @@
 WIDE = 256
 
 
-def poly_kernel(gram_ref, matrix_ref, out_ref, *buffers):
+def poly_kernel(
+    gram_ref,
+    matrix_ref,
+    branch_ref,
+    normed_ref,
+    normalized_ref,
+    inverse_std_ref,
+    vector_ref,
+    tokens_ref,
+    cotangent_ref,
+    pick_branch_ref,
+    pick_token_ref,
+    update_ref,
+    output_ref,
+    input_grad_ref,
+    vector_sum_ref,
+    own_update,
+    whole_branch,
+    whole_token,
+    out_branch,
+    in_branch,
+    out_token,
+    in_token,
+    wide,
+    *buffers,
+):
+    at = Place()
+    sems, buffers = buffers[8:], buffers[:8]
+    spread_branch = RowSpread(at, whole_branch, sems[0:4])
+    spread_token = RowSpread(at, whole_token, sems[4:8])
+    swap_branch = ColSwap(at, lambda c: out_branch.at[c], lambda c: in_branch.at[c], sems[8:10])
+    swap_token = ColSwap(at, lambda c: out_token.at[c], lambda c: in_token.at[c], sems[10:12])
+    feats = out_branch.shape[2]
+    swap_update = ColSwap(
+        at,
+        lambda c: own_update.at[pl.ds(c * feats, feats), :],
+        lambda c: update_ref.at[c],
+        sems[12:14],
+    )
+    piece, stride = out_branch.shape[1], out_token.shape[1]
+    meet(row_peers(at) + col_peers(at))
+
+    lanes = [slice(f * feats, (f + 1) * feats) for f in range(at.cols)]
+    for f in range(at.cols):
+        out_branch[f] = branch_ref[:, lanes[f]]
+    swap_branch.start()
+    in_branch[at.col] = out_branch[at.col]
+    width = at.cols * feats
+    scaled = [normed_ref[:, lanes[f]] * vector_ref[f][0:1, :] for f in range(at.cols)]
+    mean_first = sum(jnp.sum(part, axis=1, keepdims=True) for part in scaled) / width
+    mean_second = (
+        sum(
+            jnp.sum(part * normalized_ref[:, lanes[f]], axis=1, keepdims=True)
+            for f, part in enumerate(scaled)
+        )
+        / width
+    )
+    for f in range(at.cols):
+        normalized, grad = normalized_ref[:, lanes[f]], normed_ref[:, lanes[f]]
+        token_grad = inverse_std_ref[...] * (scaled[f] - mean_first - normalized * mean_second)
+        out_token[f, :piece, :] = token_grad.astype(bf16)
+        gain_grad = jnp.sum(grad * normalized, axis=0, keepdims=True)
+        shift_grad = jnp.sum(grad, axis=0, keepdims=True)
+        sums = jnp.concatenate(
+            [part.astype(f32) for part in (*split(gain_grad), *split(shift_grad))]
+            + [jnp.zeros((stride - piece - 4, feats), f32)],
+            axis=0,
+        )
+        out_token[f, piece:, :] = sums.astype(bf16)
+    swap_token.start()
+    in_token[at.col] = out_token[at.col]
+    cot_sum = jnp.sum(cotangent_ref[...].astype(f32), axis=0, keepdims=True)
+    cot_rows = jnp.concatenate(
+        [part.astype(f32) for part in split(cot_sum)] + [jnp.zeros((14, feats), f32)], axis=0
+    )
+    swap_branch.arrived()
+    for c in range(at.cols):
+        whole_branch[at.row, c * piece : (c + 1) * piece, :] = in_branch[c]
+    spread_branch.start()
+    swap_token.arrived()
+    for c in range(at.cols):
+        whole_token[at.row, c * stride : (c + 1) * stride, :] = in_token[c]
+    last = whole_token.shape[1] - 16
+    whole_token[at.row, last:, :] = cot_rows.astype(bf16)
+    spread_token.start()
+
     first, second, third, thin = [buffers[2 * i : 2 * i + 2] for i in range(4)]
     strips = matrix_ref.shape[0]
     size = strips * BLK
@@ -552,13 +1046,13 @@
             places.append((i, j, index))
             index += 1
     trace = sum(
-        jnp.sum(jnp.where(eye, gram_ref[at * BLK : (at + 1) * BLK, :], 0.0))
-        for i, j, at in places
+        jnp.sum(jnp.where(eye, gram_ref[spot * BLK : (spot + 1) * BLK, :], 0.0))
+        for i, j, spot in places
         if i == j
     )
     shrink = 1.0 / (jnp.sqrt(jnp.full((1, 1), trace, f32)) + ortho_floor)
-    for i, j, at in places:
-        block = gram_ref[at * BLK : (at + 1) * BLK, :] * (shrink * shrink)
+    for i, j, spot in places:
+        block = gram_ref[spot * BLK : (spot + 1) * BLK, :] * (shrink * shrink)
         here, there = slice(i * BLK, (i + 1) * BLK), slice(j * BLK, (j + 1) * BLK)
         put(first, here, there, block)
         if j > i:
@@ -603,7 +1097,17 @@
 
     def two(step, carry):
         sweep(first, second, third)
+
+        @pl.when(step == 1)
+        def _():
+            spread_token.middle()
+
         sweep(second, first, third)
+
+        @pl.when(step == 0)
+        def _():
+            spread_branch.middle()
+
         return carry
 
     lax.fori_loop(0, 2, two, 0)
@@ -617,43 +1121,122 @@
         put(thin, slice(i * WIDE, (i + 1) * WIDE), everything, value)
     for i, value in zip(counts, thin_product(first)):
         result = poly_linear * old[i] + poly_square * once[i] + poly_cubic * value
-        out_ref[i * WIDE : (i + 1) * WIDE, :] = result.astype(bf16)
-
-
-def orthogonalize(gram, matrix):
-    size, width = matrix.shape[0] * BLK, matrix.shape[2]
+        own_update[i * WIDE : (i + 1) * WIDE, :] = result.astype(bf16)
+    swap_update.start()
+    update_ref[at.col] = own_update[pl.ds(at.col * feats, feats), :]
+
+    held = tokens_ref.shape[0]
+
+    def choose(pick_ref, base_ref, out_ref, shift):
+        def eight(step, carry):
+            begin = step * 8
+            found = [wide[pl.ds(pick_ref[begin + i], 1), :] for i in range(8)]
+            out_ref[pl.ds(begin, 8), :] = jnp.concatenate(found, axis=0)
+            return carry
+
+        lax.fori_loop(0, held // 8, eight, 0)
+        out_ref[...] = out_ref[...] + base_ref[...].astype(f32) + shift
+
+    def widen(whole):
+        size = whole.shape[1]
+        for row in range(whole.shape[0]):
+            wide[row * size : (row + 1) * size, :] = whole[row].astype(f32)
+
+    spread_branch.finish()
+    widen(whole_branch)
+    choose(pick_branch_ref, tokens_ref, output_ref, vector_ref[at.col][2:3, :])
+    spread_token.finish()
+    widen(whole_token)
+    choose(pick_token_ref, cotangent_ref, input_grad_ref, 0.0)
+    total = jnp.zeros((16, feats), f32)
+    for row in range(whole_token.shape[0]):
+        cot_part = whole_token[row, last:, :].astype(f32)
+        for c in range(at.cols):
+            begin = c * stride + piece
+            total = total + whole_token[row, begin : begin + 16, :].astype(f32)
+        total = total + jnp.concatenate(
+            [jnp.zeros((4, feats), f32), cot_part[0:2, :], jnp.zeros((10, feats), f32)], axis=0
+        )
+    vector_sum_ref[...] = total
+    swap_update.arrived()
+    for moved in (swap_branch, swap_token, swap_update, spread_branch, spread_token):
+        moved.sent()
+
+
+def orthogonalize(
+    gram,
+    matrix,
+    branch_sum,
+    normed_sum,
+    normalized,
+    inverse_std,
+    vectors,
+    tokens,
+    cotangent,
+    picks,
+    rows,
+):
+    cols, feats, width = matrix.shape
+    size = cols * BLK
+    piece = branch_sum.shape[0]
+    stride = piece + EXTRA
+    held = tokens.shape[0]
+    chips = rows // 2
+    dma = pltpu.SemaphoreType.DMA
+    shape = jax.ShapeDtypeStruct
     square, narrow = pltpu.VMEM((size, size), bf16), pltpu.VMEM((size, width), bf16)
-    return pl.pallas_call(
+    return remote_call(
         poly_kernel,
-        out_shape=jax.ShapeDtypeStruct((size, width), bf16),
-        scratch_shapes=[*([square] * 6), *([narrow] * 2)],
-        compiler_params=pltpu.CompilerParams(vmem_limit_bytes=VMEM_LIMIT),
-        cost_estimate=pl.CostEstimate(
-            flops=48 * size**3, bytes_accessed=12 * size * size, transcendentals=0
+        3,
+        (
+            shape((cols, feats, width), bf16),
+            shape((held, feats), f32),
+            shape((held, feats), f32),
+            shape((16, feats), f32),
         ),
-        name="orthogonalize",
-    )(gram, matrix)
-
-
-def gram_all(in_part, bias, out_grad, old_momentum, rows, cols):
+        [*([VMEM_SPEC] * 9), SMEM_SPEC, SMEM_SPEC],
+        [
+            narrow,
+            pltpu.VMEM((rows, cols * piece, feats), bf16),
+            pltpu.VMEM((rows, cols * stride + 16, feats), bf16),
+            *([pltpu.VMEM((cols, piece, feats), bf16)] * 2),
+            *([pltpu.VMEM((cols, stride, feats), bf16)] * 2),
+            pltpu.VMEM((rows * (cols * stride + 16), feats), f32),
+            *([square] * 6),
+            *([narrow] * 2),
+            *([dma((chips,))] * 8),
+            *(swap_sems(cols) * 3),
+        ],
+        60 * 10**9,
+        "orthogonalize",
+    )(
+        *(gram, matrix, branch_sum, normed_sum, normalized, inverse_std, vectors),
+        *(tokens, cotangent, *picks),
+    )
+
+
+def gram_all(in_part, bias, out_grad, old_momentum, normed_part, rows, cols):
     feats, width = in_part.shape[1:]
+    full = normed_part.shape[1]
     chips = rows // 2
+    piece = normed_part.shape[0] // rows
     blocks = cols * (cols + 1) // 2
     count = chips * 2
     half_rows = blocks * BLK // 2
     shape = jax.ShapeDtypeStruct
     dma = pltpu.SemaphoreType.DMA
-    return pl.pallas_call(
+    return remote_call(
         gram_kernel,
-        out_shape=(
+        1,
+        (
             shape((feats, width), f32),
             shape(bias.shape, f32),
             shape((cols, feats, BLK), f32),
             shape((blocks * BLK, BLK), f32),
+            shape((piece, full), f32),
         ),
-        in_specs=[VMEM_SPEC] * 4,
-        out_specs=(VMEM_SPEC,) * 4,
-        scratch_shapes=[
+        [VMEM_SPEC] * 5,
+        [
             pltpu.VMEM((cols, feats, width), bf16),
             pltpu.VMEM((cols,) + bias.shape, f32),
             pltpu.VMEM((cols, feats, BLK), f32),
@@ -661,70 +1244,23 @@
             pltpu.VMEM((blocks // 2, BLK, BLK), f32),
             pltpu.VMEM((half_rows, BLK), f32),
             pltpu.VMEM((count, half_rows // count, BLK), f32),
+            *sum_scratch(piece, full, chips),
             *(swap_sems(cols) * 3),
             dma((2,)),
             dma((2,)),
             *([dma((count,))] * 4),
         ],
-        compiler_params=pltpu.CompilerParams(
-            collective_id=1, has_side_effects=True, vmem_limit_bytes=VMEM_LIMIT
-        ),
-        name="gram_all",
-    )(in_part, bias, out_grad, old_momentum)
-
-
-def attend(queries, keys_all, values_all, starts):
-    rows = queries.shape[0]
-    return pl.pallas_call(
-        attend_kernel,
-        out_shape=(
-            jax.ShapeDtypeStruct((rows, HEAD), bf16),
-            jax.ShapeDtypeStruct((rows, 1), f32),
-        ),
-        compiler_params=pltpu.CompilerParams(vmem_limit_bytes=VMEM_LIMIT),
-        cost_estimate=pl.CostEstimate(
-            flops=2 * rows * rows * HEAD, bytes_accessed=rows * 1024, transcendentals=rows * rows // 2
-        ),
-        name="attend",
-    )(queries, keys_all, values_all, starts)
-
-
-def attend_back(queries, keys_all, values_all, starts, attended, attended_grad, totals):
-    rows = queries.shape[0]
-    return pl.pallas_call(
-        attend_back_kernel,
-        out_shape=(jax.ShapeDtypeStruct((rows, HEAD), f32),) * 3,
-        compiler_params=pltpu.CompilerParams(vmem_limit_bytes=VMEM_LIMIT),
-        cost_estimate=pl.CostEstimate(
-            flops=5 * rows * rows * HEAD, bytes_accessed=rows * 4096, transcendentals=rows * rows // 2
-        ),
-        name="attend_back",
-    )(queries, keys_all, values_all, starts, attended, attended_grad, totals)
-
-
-def rotary_tables(places):
+        60 * 10**9,
+        "gram_all",
+    )(in_part, bias, out_grad, old_momentum, normed_part.reshape(chips, 2, piece, full))
+
+
+def rotary_table(places):
     half_rot = ROT // 2
     inverse = 1.0 / 10000.0 ** (jnp.arange(half_rot, dtype=f32) * (2.0 / ROT))
     angles = inverse[:, None] * places.astype(f32)[None, :]
-    return (jnp.cos(angles).T, jnp.sin(angles).T)
-
-
-def rotate(values, cosine, sine):
-    half_rot = ROT // 2
-    lower_half = values[..., :half_rot]
-    upper_half = values[..., half_rot:ROT]
-    return jnp.concatenate(
-        [
-            lower_half * cosine - upper_half * sine,
-            upper_half * cosine + lower_half * sine,
-            values[..., ROT:],
-        ],
-        axis=-1,
-    )
-
-
-def gelu_tanh(values):
-    return jax.nn.gelu(values, approximate=True)
+    table = jnp.concatenate([jnp.cos(angles), jnp.sin(angles)], axis=0)
+    return jnp.concatenate(high_low(table), axis=0)
 
 
 def adam_step(value, gradient, first_state, second_state):
@@ -733,22 +1269,6 @@
     corrected = first_new / (1.0 - beta_first**STEP)
     root_term = jnp.sqrt(second_new / (1.0 - beta_second**STEP)) + adam_floor
     return (first_new, second_new, value - rate_vector * corrected / root_term)
-
-
-def gather_row(x):
-    return lax.all_gather(x, "row", axis=0, tiled=True)
-
-
-def swap_col(x):
-    return lax.all_to_all(x, "col", split_axis=0, concat_axis=0, tiled=True)
-
-
-def sum_scatter(x, axis):
-    return lax.psum_scatter(x, axis, scatter_dimension=0, tiled=True)
-
-
-def take_rows(x, index):
-    return x.at[index].get(mode="promise_in_bounds")
 
 
 def high_low(x):
@@ -802,7 +1322,7 @@
     own = row * held + jnp.arange(held, dtype=jnp.int32)
     holds = (seq_starts[None, :] <= own[:, None]) & (own[:, None] < seq_ends[None, :])
     dealt_at = own + jnp.sum(jnp.where(holds, (dealt_starts - seq_starts)[None, :], 0), axis=1)
-    cosine, sine = rotary_tables(places)
+    table = rotary_table(places)
 
     def lanes(x, width):
         return jnp.pad(x, ((0, 0), (0, width - x.shape[1])))
@@ -823,92 +1343,23 @@
     dealt, cotangent_dealt, weight_all, vector_all, normalized, inverse_std = deal_all(
         tokens, cotangent, pick, tile, jnp.pad(norm_vectors, ((0, 5), (0, 0))), rows, cols
     )
-    in_all, out_all = weight_all[:, :in_pad], weight_all[:, in_pad:]
-    gain_all = vector_all[:, 0, :].reshape(1, D)
-
-    def deal_back(x, more, own_more):
-        parts = x.astype(bf16).reshape(piece, cols, feats).transpose(1, 0, 2)
-        if more is None:
-            stride = piece
-            swapped = swap_col(parts)
-        else:
-            stride = piece + EXTRA
-            swapped = swap_col(jnp.concatenate([parts, more], axis=1))
-            own_more = jnp.pad(
-                own_more[None], ((0, cols - 1), (stride - own_more.shape[0], 0), (0, 0))
-            )
-            swapped = swapped + own_more
-        whole = gather_row(swapped.reshape(cols * stride, feats))
-        block, inside = dealt_at // group, dealt_at % group
-        index = (inside // piece) * (cols * stride) + block * stride + inside % piece
-        return take_rows(whole, index), whole
-
-    out_bias = norm_vectors[2]
-    preact = dot_nn(dealt, in_all)
-    pre_qkv = preact[:, :qkv_width] + qkv_bias
-    pre_up = preact[:, up_width:] + mlp_bias
-    queries = (rotate(pre_qkv[:, :HEAD], cosine, sine).astype(bf16) * HEAD**-0.5).astype(bf16)
-    keys_all = rotate(pre_qkv[:, HEAD : 2 * HEAD], cosine, sine).astype(bf16)
-    values_all = pre_qkv[:, 2 * HEAD :].astype(bf16)
-    attended, totals = attend(queries, keys_all, values_all, starts)
-    activated, gelu_back = jax.vjp(gelu_tanh, pre_up)
-    branch = jnp.concatenate([lanes(attended, 128), activated.astype(bf16)], axis=1)
-    branch_sum = sum_scatter(dot_nt(branch, out_all).astype(bf16), "row")
-    branch_back, _ = deal_back(branch_sum, None, None)
-    output = tokens.astype(f32) + branch_back.astype(f32) + out_bias
-
-    branch_grad = dot_nn(cotangent_dealt, out_all)
-    out_grad = sum_scatter(dot_tn(cotangent_dealt, branch), "col")
-    attended_grad = branch_grad[:, :proj_width].astype(bf16)
-    up_pre_grad = gelu_back(branch_grad[:, 128:])[0]
-    query_grad, key_grad, value_grad = attend_back(
-        queries, keys_all, values_all, starts, attended, attended_grad, totals
-    )
-    preact_grad = jnp.concatenate(
-        [
-            rotate(query_grad, cosine, -sine),
-            rotate(key_grad, cosine, -sine),
-            value_grad,
-            jnp.zeros_like(value_grad),
-            up_pre_grad,
-        ],
-        axis=1,
-    ).astype(bf16)
-    in_part = dot_tn(dealt, preact_grad).astype(bf16).reshape(cols, feats, in_pad)
-    bias_part = jnp.sum(preact_grad, axis=0, dtype=f32)
-    normed_grad = sum_scatter(dot_nt(preact_grad, in_all).astype(bf16), "row").astype(f32)
-    scaled = normed_grad * gain_all
-    mean_first = jnp.mean(scaled, axis=1, keepdims=True)
-    mean_second = jnp.mean(scaled * normalized, axis=1, keepdims=True)
-    token_grad = inverse_std * (scaled - mean_first - normalized * mean_second)
-    vector_rows = jnp.stack(
-        [
-            *high_low(jnp.sum(normed_grad * normalized, axis=0)),
-            *high_low(jnp.sum(normed_grad, axis=0)),
-        ],
-        axis=0,
-    )
-    vector_rows = jnp.pad(
-        vector_rows.reshape(4, cols, feats).transpose(1, 0, 2), ((0, 0), (0, EXTRA - 4), (0, 0))
-    )
-    bias_rows = jnp.stack(high_low(jnp.sum(cotangent, axis=0, dtype=f32)), axis=0)
-    token_back, whole = deal_back(token_grad, vector_rows, bias_rows)
-    input_grad = cotangent.astype(f32) + token_back.astype(f32)
-    vector_sum = jnp.sum(
-        whole.reshape(rows * cols, piece + EXTRA, feats)[:, piece:].astype(f32), axis=0
-    )
-    norm_grads = jnp.stack(
-        [
-            vector_sum[0] + vector_sum[1],
-            vector_sum[2] + vector_sum[3],
-            vector_sum[-2] + vector_sum[-1],
-        ],
-        axis=0,
-    )
-
-    out_grad = jnp.concatenate(
-        [lanes(out_grad[:, :proj_width], up_width), out_grad[:, 128:]], axis=1
-    )
+
+    block, inside = dealt_at // group, dealt_at % group
+    inner = inside % piece
+    stride = piece + EXTRA
+    pick_branch = (inside // piece) * (cols * piece) + block * piece + inner
+    pick_token = (inside // piece) * (cols * stride + 16) + block * stride + inner
+
+    bias = jnp.concatenate(
+        [jnp.pad(qkv_bias, (0, up_width - qkv_width)), mlp_bias], axis=0
+    ).reshape(1, in_pad)
+    *kept, branch_part, out_part = forward(
+        dealt, cotangent_dealt, weight_all, bias, table, starts
+    )
+    in_part, bias_part, normed_part, branch_sum, out_grad = backward(
+        dealt, cotangent_dealt, weight_all, table, starts, kept, branch_part, out_part, rows, cols
+    )
+
     old_momentum = jnp.concatenate(
         [
             lanes(qkv_momentum, up_width),
@@ -918,8 +1369,29 @@
         ],
         axis=1,
     )
-    in_grad, bias_rows, matrix, gram = gram_all(
-        in_part, jnp.broadcast_to(bias_part[None], (8, in_pad)), out_grad, old_momentum, rows, cols
+    in_grad, bias_rows, matrix, gram, normed_sum = gram_all(
+        in_part, bias_part, out_grad, old_momentum, normed_part, rows, cols
+    )
+    returned, output, input_grad, vector_sum = orthogonalize(
+        gram,
+        matrix,
+        branch_sum,
+        normed_sum,
+        normalized,
+        inverse_std,
+        vector_all,
+        tokens,
+        cotangent,
+        (pick_branch, pick_token),
+        rows,
+    )
+    norm_grads = jnp.stack(
+        [
+            vector_sum[0] + vector_sum[1],
+            vector_sum[2] + vector_sum[3],
+            vector_sum[4] + vector_sum[5],
+        ],
+        axis=0,
     )
     in_bias_grad = bias_rows[0]
     gradients = (
@@ -933,7 +1405,6 @@
     widths = (3 * D, FF, D, FF)
     sizes = (qkv_width, up_width, proj_width, up_width)
     states = [momentum * old + g for old, g in zip(old_states, gradients)]
-    returned = swap_col(orthogonalize(gram, matrix).reshape(cols, feats, BLK))
     new_weights = []
     for index in range(4):
         update = jnp.concatenate([returned[2 * index], returned[2 * index + 1]], axis=1)

time: 588 us -> 438 us (0.74)
  waiting for transfers between devices: 125 us -> 0 us
  Pallas kernels: 286 us -> 402 us
  other arithmetic: 43.7 us -> 5.43 us
  matrix products: 32.9 us -> 0 us
  local copies, waits for them, and re-layouts: 55.6 us -> 25.5 us
  between operations: 15.1 us -> 1.57 us
  blocking collectives: 11.5 us -> 0 us
  starting transfers between devices: 10.9 us -> 0 us
    pallas_call x4, Pallas kernels: 143 us -> 281 us  [the longest x1 107 us: orthogonalize(): remote_call(poly_kernel, 3, (shape((cols, feats, width), bf16), shape((he...]
    reduce_scatter x3 -> x0, waiting for transfers between devices: 116 us -> none  [sum_scatter(): return lax.psum_scatter(x, axis, scatter_dimension=0, tiled=True)]
    dot_general x6 -> x0, matrix products: 32.9 us -> none  [the longest x2 11.5 us: dot_nn(): lax.dot_general(a, b, (((1,), (0,)), ((), ())), preferred_element_type=f3...]
    pallas_call x1, Pallas kernels: 142 us -> 121 us  [deal_all(): pl.pallas_call(deal_kernel, out_shape=(shape((group, width), bf16), shape...]
    mul x8 -> x0, local copies, waits for them, and re-layouts: 11.9 us -> none  [the longest x2 4.4 us: rotate(): lower_half * cosine - upper_half * sine]
    all_to_all x1 -> x0, blocking collectives: 11.5 us -> none  [swap_col(): return lax.all_to_all(x, 'col', split_axis=0, concat_axis=0, tiled=True)]
    gather x2 -> x0, local copies, waits for them, and re-layouts: 11.4 us -> none  [take_rows(): return x.at[index].get(mode='promise_in_bounds')]
    all_to_all x2 -> x0, starting transfers between devices: 9.86 us -> none  [swap_col(): return lax.all_to_all(x, 'col', split_axis=0, concat_axis=0, tiled=True)]
  transfers between devices with their start and end apart: 7 -> 0, of which waited for: 5 -> 0; matrix products, arithmetic and copies ran while one was open for 13% -> 0% of each run, Pallas kernels for 24% -> 0%
where the time goes in v3:
time: 438 us; the launch traced here: 434 us
  Pallas kernels  402 us (92%)
  local copies, waits for them, and re-layouts  25.5 us (6%)
  other arithmetic  5.43 us (1%)
    pallas_call x1, Pallas kernels, deal_all(): pl.pallas_call(deal_kernel, out_shape=(shape((group, width), bf16), shape...  121 us
    pallas_call x1, Pallas kernels, orthogonalize(): remote_call(poly_kernel, 3, (shape((cols, feats, width), bf16), shape((he...  107 us
    pallas_call x1, Pallas kernels, gram_all(): remote_call(gram_kernel, 1, (shape((feats, width), f32), shape(bias.shape...  93.7 us
    pallas_call x1, Pallas kernels, backward(): remote_call(backward_kernel, 2, (shape((cols, feats, in_width), bf16), sh...  60.1 us
    unnamed x107, local copies, waits for them, and re-layouts  22.5 us
    pallas_call x1, Pallas kernels, forward(): local_call(forward_kernel, (*(head, head, head), shape((rows, up), f32),...  21 us

profile of v3, /device:TPU:0, one launch (start us, length us, event | category | flops | bytes accessed | tf_op | source)
XLA Modules:
  0.0 434.4 jit_solution(7095148469508333194)
XLA Ops:
  0.7 0.8 dynamic_slice.7
  2.5 0.8 select_reduce_fusion.1
  4.7 0.8 constant_dynamic-slice_fusion
  6.1 120.7 %deal_all.1 = (bf16[2048,1024]{1,0:T(8,128)(2,1)}, bf16[2048,1024]{1,0:T(8,128)(2,1)}, bf16[1024,896]{1,0:T(8,128)(2,1)S(1)}, f32[8,8,128]{2,1,0:T(8,128)S(1)}, ...) custom-call(bf16[1024,128]{1,0:T(8,128)(2,1)S(1)} %copy-done, bf16[1024,128]{1,0:T(8,128)(2,1)S(1)} %copy-done.1, ...), custom_call_target="tpu_custom_call" | custom-call | flops 99999997952 | bytes 16777216 | tf_op jit(solution)/shard_map/deal_all/pallas_call | solution.py:747
  126.8 1.2 copy-done.2
  128.0 0.8 copy-done.10
  128.8 21.0 %forward.1 = (bf16[2048,64]{1,0:T(8,128)(2,1)S(1)}, bf16[2048,64]{1,0:T(8,128)(2,1)S(1)}, bf16[2048,64]{1,0:T(8,128)(2,1)S(1)}, f32[2048,256]{1,0:T(8,128)}, bf1...) custom-call(bf16[2048,1024]{1,0:T(8,128)(2,1)} %get-tuple-element.51.dealt, ...), custom_call_target="tpu_custom_call" | custom-call | flops 24999999488 | bytes 16777216 | tf_op jit(solution)/shard_map/forward/pallas_call | solution.py:236
  149.8 1.1 copy-done.3
  150.9 60.1 %backward.1 = (bf16[8,128,512]{2,1,0:T(8,128)(2,1)S(1)}, f32[8,512]{1,0:T(8,128)S(1)}, bf16[2048,1024]{1,0:T(8,128)(2,1)}, bf16[128,1024]{1,0:T(8,128)(2,1)S(1)}, f32[128,512]{1,0:T(8,128)S(1)}) custom-call(bf16[2048,1024]{1,0:T(8,128)(2,1)} %get-tuple-element.51.dealt_ref, bf16[2048,1024]{1,0:T(8,128)(2,1)} %get-tuple-element.52.cotangent_ref, ...), custom_call_target="tpu_custom_call" | custom-call | flops 30000001024 | bytes 16777216 | tf_op jit(solution)/shard_map/backward/pallas_call | solution.py:273
  211.0 1.0 copy.122
  212.0 1.0 copy.120
  213.1 0.9 copy.121
  214.1 93.7 %gram_all.1 = (f32[128,512]{1,0:T(8,128)S(1)}, f32[8,512]{1,0:T(8,128)S(1)}, f32[8,128,128]{2,1,0:T(8,128)S(1)}, f32[4608,128]{1,0:T(8,128)S(1)}, f32[128,1024]{1,0:T(8,128)S(1)}) custom-call(bf16[8,128,512]{2,1,0:T(8,128)(2,1)S(1)} %get-tuple-element.62.in_part_ref, f32[8,512]{1,0:T(8,128)S(1)} %get-tuple-element.63.bias_ref, ...), custom_call_target="tpu_custom_call" | custom-call | flops 60000002048 | bytes 16777216 | tf_op jit(solution)/shard_map/gram_all/pallas_call | solution.py:1228
  307.8 1.4 copy-done.4
  309.2 0.8 copy-done.6
  310.0 0.8 copy-done.8
  311.5 1.7 copy-done.5
  313.1 1.0 copy-done.7
  314.2 1.0 copy-done.9
  315.2 1.0 copy-done.11
  316.3 106.6 %orthogonalize.1 = (bf16[8,128,128]{2,1,0:T(8,128)(2,1)S(1)}, f32[1024,128]{1,0:T(8,128)S(1)}, f32[1024,128]{1,0:T(8,128)S(1)}, f32[16,128]{1,0:T(8,128)S(1)}) custom-call(f32[4608,128]{1,0:T(8,128)S(1)} %copy-done.5, f32[8,128,128]{2,1,0:T(8,128)S(1)} %copy-done.7, bf16[128,1024]{1,0:T(8,128)(2,1)S(1)} %get-tuple-element.68.branch_ref, ...), custom_call_target="tpu_custom_call" | custom-call | flops 60000002048 | bytes 16777216 | tf_op jit(solution)/shard_map/orthogonalize/pallas_call | solution.py:1188
  425.4 0.8 multiply_add_fusion.1
  432.6 0.8 copy.140
  433.4 0.8 copy.141
  (133 shorter events, 12.3 us)
Async XLA Ops:
  0.7 5.3 %copy-start = (bf16[1024,128]{1,0:T(8,128)(2,1)S(1)}, bf16[1024,128]{1,0:T(8,128)(2,1)}, u32[]{:S(2)}) copy-start(bf16[1024,128]{1,0:T(8,128)(2,1)} %tokens_ref.3) | copy-start | bytes 786436
  5.6 121.2 %copy-start.16 = (f32[256,128]{0,1:T(8,128)}, f32[256,128]{0,1:T(8,128)S(1)}, u32[]{:S(2)}) copy-start(f32[256,128]{0,1:T(8,128)S(1)} %copy.116) | copy-start | bytes 393220
  6.0 122.8 %copy-start.34 = (f32[192]{0:T(256)S(1)}, f32[192]{0:T(256)}, u32[]{:S(2)}) copy-start(f32[192]{0:T(256)} %param.30) | copy-start | bytes 2308
  6.0 122.8 %copy-start.36 = (f32[256]{0:T(256)S(1)}, f32[256]{0:T(256)}, u32[]{:S(2)}) copy-start(f32[256]{0:T(256)} %param.31) | copy-start | bytes 3076
  150.9 63.1 %copy-start.20 = (f32[128,256]{1,0:T(8,128)S(1)}, f32[128,256]{1,0:T(8,128)}, u32[]{:S(2)}) copy-start(f32[128,256]{1,0:T(8,128)} %param.33) | copy-start | bytes 393220
  213.9 93.8 %copy-start.18 = (f32[64,128]{0,1:T(8,128)}, f32[64,128]{0,1:T(8,128)S(1)}, u32[]{:S(2)}) copy-start(f32[64,128]{0,1:T(8,128)S(1)} %copy.121) | copy-start | bytes 98308
  214.0 96.8 %copy-start.33 = (s32[32]{0:T(128)S(1)}, s32[32]{0:T(128)}, u32[]{:S(2)}) copy-start(s32[32]{0:T(128)} %copy-done.32) | copy-start | bytes 388
  214.1 96.7 %copy-start.40 = (s32[32]{0:T(128)S(1)}, s32[32]{0:T(128)}, u32[]{:S(2)}) copy-start(s32[32]{0:T(128)} %param.23) | copy-start | bytes 388
  214.1 96.7 %copy-start.29 = (s32[16384]{0:T(1024)S(1)}, s32[16384]{0:T(1024)}, u32[]{:S(2)}) copy-start(s32[16384]{0:T(1024)} %param.24) | copy-start | bytes 196612
  316.3 106.7 %copy-start.31 = (f32[3,128]{1,0:T(4,128)S(1)}, f32[3,128]{1,0:T(4,128)}, u32[]{:S(2)}) copy-start(f32[3,128]{1,0:T(4,128)} %param.29) | copy-start | bytes 4612
  316.3 106.8 %copy-start.38 = (f32[3,128]{1,0:T(4,128)S(1)}, f32[3,128]{1,0:T(4,128)}, u32[]{:S(2)}) copy-start(f32[3,128]{1,0:T(4,128)} %param.37) | copy-start | bytes 4612
  316.3 106.8 %copy-start.39 = (f32[3,128]{1,0:T(4,128)S(1)}, f32[3,128]{1,0:T(4,128)}, u32[]{:S(2)}) copy-start(f32[3,128]{1,0:T(4,128)} %param.36) | copy-start | bytes 4612
  316.3 107.4 %copy-start.17 = (f32[256,128]{0,1:T(8,128)S(1)}, f32[256,128]{0,1:T(8,128)}, u32[]{:S(2)}) copy-start(f32[256,128]{0,1:T(8,128)} %copy-done.16) | copy-start | bytes 393220
  316.3 108.2 %copy-start.25 = (f32[128,192]{0,1:T(8,128)S(1)}, f32[128,192]{0,1:T(8,128)}, u32[]{:S(2)}) copy-start(f32[128,192]{0,1:T(8,128)} %param.25) | copy-start | bytes 294916
  316.3 109.1 %copy-start.21 = (f32[128,256]{1,0:T(8,128)S(1)}, f32[128,256]{1,0:T(8,128)}, u32[]{:S(2)}) copy-start(f32[128,256]{1,0:T(8,128)} %param.33) | copy-start | bytes 393220
  316.3 109.0 %copy-start.23 = (f32[128,256]{1,0:T(8,128)S(1)}, f32[128,256]{1,0:T(8,128)}, u32[]{:S(2)}) copy-start(f32[128,256]{1,0:T(8,128)} %param.26) | copy-start | bytes 393220
  422.9 5.5 %copy-start.35 = (f32[192]{0:T(256)S(1)}, f32[192]{0:T(256)}, u32[]{:S(2)}) copy-start(f32[192]{0:T(256)} %param.30) | copy-start | bytes 2308
  422.9 5.5 %copy-start.41 = (f32[192]{0:T(256)S(1)}, f32[192]{0:T(256)}, u32[]{:S(2)}) copy-start(f32[192]{0:T(256)} %param.39) | copy-start | bytes 2308
  422.9 5.5 %copy-start.42 = (f32[192]{0:T(256)S(1)}, f32[192]{0:T(256)}, u32[]{:S(2)}) copy-start(f32[192]{0:T(256)} %param.38) | copy-start | bytes 2308
  423.0 6.1 %copy-start.37 = (f32[256]{0:T(256)S(1)}, f32[256]{0:T(256)}, u32[]{:S(2)}) copy-start(f32[256]{0:T(256)} %param.31) | copy-start | bytes 3076
  423.0 6.1 %copy-start.43 = (f32[256]{0:T(256)S(1)}, f32[256]{0:T(256)}, u32[]{:S(2)}) copy-start(f32[256]{0:T(256)} %param.41) | copy-start | bytes 3076
  423.0 6.1 %copy-start.44 = (f32[256]{0:T(256)S(1)}, f32[256]{0:T(256)}, u32[]{:S(2)}) copy-start(f32[256]{0:T(256)} %param.40) | copy-start | bytes 3076
  423.0 6.7 %copy-start.13 = (f32[256,128]{0,1:T(8,128)S(1)}, f32[256,128]{0,1:T(8,128)}, u32[]{:S(2)}) copy-start(f32[256,128]{0,1:T(8,128)} %copy-done.12) | copy-start | bytes 393220
  424.5 6.7 %copy-start.19 = (f32[64,128]{0,1:T(8,128)S(1)}, f32[64,128]{0,1:T(8,128)}, u32[]{:S(2)}) copy-start(f32[64,128]{0,1:T(8,128)} %copy-done.18) | copy-start | bytes 98308
  (21 other events, 54.9 us)
